TPU v7x, 32 devices: a whole 2x2x4 slice. The times are simulated.
32 devices in a mesh: face: 2 (over y), tile: 16 (over z, x, core).
Axes of the slice: x: 2, y: 2, z: 4, core: 2. Of those that a mesh axis runs over, the one named last changes fastest.
Arguments:
- state_field: bfloat16 [96, 768, 128], P('face', 'tile'), may hold values from -6 to 6
- turn_codes: int32 [2, 16, 4], P('face', 'tile'), may hold values from 0 to 3
- depth_kernel: float32 [7, 7, 128], replicated, may hold values from -0.875 to 0.875
- conv_bias: float32 [128], replicated, may hold values from -3 to 3
- norm_gain: float32 [128], replicated, may hold values from 0.5 to 1.5
- norm_shift: float32 [128], replicated, may hold values from -2 to 2
- weight_in: bfloat16 [128, 512], replicated, may hold values from -0.5 to 0.5
- bias_in: float32 [512], replicated, may hold values from -3 to 3
- weight_out: bfloat16 [512, 128], replicated, may hold values from -0.25 to 0.25
- bias_out: float32 [128], replicated, may hold values from -3 to 3
- layer_scale: float32 [128], replicated, may hold values from 0.5 to 1.5
- cotangent: bfloat16 [96, 768, 128], P('face', 'tile'), may hold values from -6 to 6
Outputs:
- block_out: bfloat16 [96, 768, 128], P('face', 'tile')
- grad_field: bfloat16 [96, 768, 128], P('face', 'tile')
- grad_weight_in: float32 [128, 512], replicated
- grad_weight_out: float32 [512, 128], replicated
- grad_kernel: float32 [7, 7, 128], replicated
Inputs may be any that keep to these rules, and one draw needn't show every extreme that they name: `turn_codes`: quarter turn counts; for the south and north strips only their parity acts.
All inputs are finite; a program needn't handle non-finite values.
Results may differ from a plain program's by a relative error of at most 0.0067.
Values may be sent and summed in bfloat16 or wider, within the bound.
A program may use at most 64 MiB of HBM per device.

v0:
```python
import math

import jax
import jax.numpy as jnp
from jax import lax
from jax.sharding import PartitionSpec as P


def as_sent(value):
    return jax.tree.map(lambda a: a.astype(jnp.bfloat16) if a.dtype == jnp.float32 else a, value)


def extended(value, sides, width):
    for axis, dim in sides:
        size, length = (lax.axis_size(axis), value.shape[dim])
        up = [(i, (i + 1) % size) for i in range(size)]
        down = [(j, i) for i, j in up]
        last = lax.slice_in_dim(value, length - width, length, axis=dim)
        initial = lax.slice_in_dim(value, 0, width, axis=dim)
        before = lax.ppermute(last, axis, up)
        after = lax.ppermute(initial, axis, down)
        value = jnp.concatenate([before, value, after], axis=dim)
    return value


def rotate(array_in, quarters):
    return jnp.rot90(array_in, quarters, axes=(array_in.ndim - 3, array_in.ndim - 2))


def choose(options, turn_code):
    turn_code = turn_code.reshape(turn_code.shape + (1, 1, 1))
    picked = options[0]
    for option in range(1, len(options)):
        picked = jnp.where(turn_code == option, options[option], picked)
    return picked


def side_strips(tile_in, east_turn, west_turn, margin):
    tile_side = tile_in.shape[-2]
    edge_list = [
        tile_in[..., :, tile_side - margin :, :],
        tile_in[..., tile_side - margin :, :, :],
        tile_in[..., :, :margin, :],
        tile_in[..., :margin, :, :],
    ]
    east_strip = choose([rotate(edge_list[quarter], quarter) for quarter in range(4)], east_turn)
    west_strip = choose(
        [rotate(edge_list[(quarter + 2) % 4], quarter) for quarter in range(4)], west_turn
    )
    return (west_strip, east_strip)


def end_rows(widened, south_turn, north_turn, margin):
    top_rows = widened[..., :margin, :, :]
    bottom_rows = widened[..., widened.shape[-3] - margin :, :, :]
    south_strip = choose([bottom_rows, rotate(top_rows, 2)], south_turn % 2)
    north_strip = choose([top_rows, rotate(bottom_rows, 2)], north_turn % 2)
    return (north_strip, south_strip)


def tile_step(
    padded,
    tile_in,
    cotangent,
    depth_kernel,
    conv_bias,
    norm_gain,
    norm_shift,
    weight_in,
    bias_in,
    weight_out,
    bias_out,
    layer_scale,
):
    tile_side = tile_in.shape[0]
    kernel_side = depth_kernel.shape[0]
    channels = tile_in.shape[2]
    padded_f = padded.astype(jnp.float32)
    convolved = jnp.zeros(tile_in.shape, jnp.float32)
    for row_off in range(kernel_side):
        for col_off in range(kernel_side):
            convolved = (
                convolved
                + padded_f[row_off : row_off + tile_side, col_off : col_off + tile_side]
                * depth_kernel[row_off, col_off]
            )
    convolved = convolved + conv_bias
    center = convolved - jnp.mean(convolved, axis=-1, keepdims=True)
    inverse = lax.rsqrt(jnp.mean(center * center, axis=-1, keepdims=True) + 1e-06)
    normed = center * inverse
    norm_rows = (normed * norm_gain + norm_shift).astype(jnp.bfloat16).reshape(-1, channels)
    hidden = jnp.dot(norm_rows, weight_in, preferred_element_type=jnp.float32) + bias_in
    normal_cdf = 0.5 * (1.0 + lax.erf(hidden * 0.7071067811865476))
    normal_pdf = jnp.exp(-0.5 * hidden * hidden) * 0.3989422804014327
    active = (hidden * normal_cdf).astype(jnp.bfloat16)
    mixed_out = jnp.dot(active, weight_out, preferred_element_type=jnp.float32) + bias_out
    result = (tile_in.astype(jnp.float32) + layer_scale * mixed_out.reshape(tile_in.shape)).astype(
        jnp.bfloat16
    )
    grad_mixed = (
        (cotangent.astype(jnp.float32) * layer_scale).astype(jnp.bfloat16).reshape(-1, channels)
    )
    grad_out = jnp.dot(active.T, grad_mixed, preferred_element_type=jnp.float32)
    grad_active = jnp.dot(grad_mixed, weight_out.T, preferred_element_type=jnp.float32)
    grad_hidden = (grad_active * (normal_cdf + hidden * normal_pdf)).astype(jnp.bfloat16)
    grad_in = jnp.dot(norm_rows.T, grad_hidden, preferred_element_type=jnp.float32)
    grad_normed = (
        jnp.dot(grad_hidden, weight_in.T, preferred_element_type=jnp.float32).reshape(tile_in.shape)
        * norm_gain
    )
    grad_conv = inverse * (
        grad_normed
        - jnp.mean(grad_normed, axis=-1, keepdims=True)
        - normed * jnp.mean(grad_normed * normed, axis=-1, keepdims=True)
    )
    spread_by = kernel_side - 1
    grad_spread = jnp.pad(grad_conv, ((spread_by, spread_by), (spread_by, spread_by), (0, 0)))
    pad_side = tile_side + spread_by
    pad_grad = jnp.zeros((pad_side, pad_side, channels), jnp.float32)
    kernel_rows = []
    for row_off in range(kernel_side):
        for col_off in range(kernel_side):
            pad_grad = (
                pad_grad
                + grad_spread[
                    spread_by - row_off : spread_by - row_off + pad_side,
                    spread_by - col_off : spread_by - col_off + pad_side,
                ]
                * depth_kernel[row_off, col_off]
            )
            kernel_rows.append(
                jnp.sum(
                    padded_f[row_off : row_off + tile_side, col_off : col_off + tile_side]
                    * grad_conv,
                    axis=(0, 1),
                )
            )
    grad_kern = jnp.stack(kernel_rows).reshape(kernel_side, kernel_side, channels)
    return (result, pad_grad, grad_in, grad_out, grad_kern)


def body(
    state_field,
    turn_codes,
    depth_kernel,
    conv_bias,
    norm_gain,
    norm_shift,
    weight_in,
    bias_in,
    weight_out,
    bias_out,
    layer_scale,
    cotangent,
):
    tile_side = state_field.shape[0]
    margin = depth_kernel.shape[0] // 2
    turn_code = turn_codes[0, 0]
    west_strip, east_strip = side_strips(state_field, turn_code[0], turn_code[1], margin)
    side_rims = extended(
        as_sent(jnp.concatenate([west_strip, east_strip], axis=1)), (("tile", 1),), margin
    )
    widened = jnp.concatenate(
        [side_rims[:, :margin], state_field, side_rims[:, side_rims.shape[1] - margin :]], axis=1
    )
    north_strip, south_strip = end_rows(widened, turn_code[2], turn_code[3], margin)
    end_rims = extended(
        as_sent(jnp.concatenate([north_strip, south_strip], axis=0)), (("face", 0),), margin
    )
    padded = jnp.concatenate(
        [end_rims[:margin], widened, end_rims[end_rims.shape[0] - margin :]], axis=0
    )
    block_out, pad_grad, grad_in, grad_out, grad_kern = tile_step(
        padded,
        state_field,
        cotangent,
        depth_kernel,
        conv_bias,
        norm_gain,
        norm_shift,
        weight_in,
        bias_in,
        weight_out,
        bias_out,
        layer_scale,
    )
    pad_side = pad_grad.shape[0]
    back_rows = extended(
        jnp.concatenate([pad_grad[:margin], pad_grad[pad_side - margin :]], axis=0).astype(
            jnp.bfloat16
        ),
        (("face", 0),),
        margin,
    ).astype(jnp.float32)
    grad_north = back_rows[:margin]
    grad_south = back_rows[back_rows.shape[0] - margin :]
    north_half = turn_code[3] % 2
    south_half = turn_code[2] % 2
    top_add = jnp.where(north_half == 0, grad_north, 0.0) + jnp.where(
        south_half == 1, rotate(grad_south, 2), 0.0
    )
    bottom_add = jnp.where(north_half == 1, rotate(grad_north, 2), 0.0) + jnp.where(
        south_half == 0, grad_south, 0.0
    )
    grad_wide = pad_grad[margin : pad_side - margin]
    grad_wide = grad_wide.at[:margin].add(top_add).at[tile_side - margin :].add(bottom_add)
    back_cols = extended(
        jnp.concatenate([grad_wide[:, :margin], grad_wide[:, pad_side - margin :]], axis=1).astype(
            jnp.bfloat16
        ),
        (("tile", 1),),
        margin,
    ).astype(jnp.float32)
    grad_west = back_cols[:, :margin]
    grad_east = back_cols[:, back_cols.shape[1] - margin :]
    edge_grads = [0.0, 0.0, 0.0, 0.0]
    for quarter in range(4):
        edge_grads[quarter] = edge_grads[quarter] + jnp.where(
            turn_code[0] == quarter, rotate(grad_east, -quarter), 0.0
        )
        edge_grads[(quarter + 2) % 4] = edge_grads[(quarter + 2) % 4] + jnp.where(
            turn_code[1] == quarter, rotate(grad_west, -quarter), 0.0
        )
    grad_cells = grad_wide[:, margin : pad_side - margin]
    grad_cells = grad_cells.at[:, tile_side - margin :].add(edge_grads[0])
    grad_cells = grad_cells.at[tile_side - margin :].add(edge_grads[1])
    grad_cells = grad_cells.at[:, :margin].add(edge_grads[2])
    grad_cells = grad_cells.at[:margin].add(edge_grads[3])
    grad_field = (cotangent.astype(jnp.float32) + grad_cells).astype(jnp.bfloat16)
    grad_in, grad_out, grad_kern = lax.psum((grad_in, grad_out, grad_kern), ("face", "tile"))
    scale_factor = 1.0 / math.sqrt(
        tile_side * tile_side * lax.axis_size("face") * lax.axis_size("tile")
    )
    return (
        block_out,
        grad_field,
        grad_in * scale_factor,
        grad_out * scale_factor,
        grad_kern * scale_factor,
    )


def solution(mesh):
    placed = (
        P("face", "tile", None),
        P("face", "tile", None),
        P(),
        P(),
        P(),
        P(),
        P(),
        P(),
        P(),
        P(),
        P(),
        P("face", "tile", None),
    )
    return jax.shard_map(
        body,
        mesh=mesh,
        in_specs=placed,
        out_specs=(P("face", "tile", None), P("face", "tile", None), P(), P(), P()),
        check_vma=False,
    )
```

profile of v0, /device:TPU:0, one launch (start us, length us, event | category | flops | bytes accessed | tf_op | source)
XLA Modules:
  0.0 267.5 jit_solution(12691110291863553198)
XLA Ops:
  7.2 1.4 fusion.125
  16.4 5.0 %collective-permute-start.1 = (bf16[48,3,128]{2,1,0:T(4,128)(2,1)S(1)}, bf16[48,3,128]{2,1,0:T(4,128)(2,1)S(1)}, u32[]{:S(2)}, u32[]{:S(2)}) collective-permute-start(bf16[48,3,128]{2,1,0:T(4,128)(2,1)S(1)} %get-tuple-element.146), channel_id=1, source_target_pairs={{1,0},{2,1},{3,2},{4,3},{5,4},{6,5},{7,6},{8,7},{9,8},{10,9},{11,1... | collective-permute-start | bytes 110600 | tf_op jit(solution)/shard_map/ppermute | solution.py:21
  26.3 2.0 collective-permute-start.3
  30.6 1.7 collective-permute-done.2
  33.0 8.8 %fusion.119 = (f32[48,48]{1,0:T(8,128)S(1)}, f32[48,48,128]{2,1,0:T(8,128)S(1)}) fusion(f32[128]{0:T(128)S(1)} %copy-done.103, f32[128]{0:T(128)S(1)} %copy-done.59, f32[54,54,128]{2,1,0:T(8,128)S(1)} %maximum_convert_fusion, f32[128]{0:T(128)S(1)} %copy-done.60, f32[128]{0:T(128)S(1)} %get-tuple-element.156, f32[128]{0:T(128)S(1)} %get-tuple-element.157, ...), kind=kLoop, calls=%fused_computation.317 | loop fusion | flops 29193984 | bytes 59017216 | tf_op jit(solution)/shard_map/reduce_sum | solution.py:88
  43.4 1.5 multiply_convert_fusion
  47.1 1.5 fusion.127
  48.6 2.2 fusion.4
  50.9 1.8 multiply_reduce_fusion.50
  52.8 2.3 multiply_reduce_fusion.49
  55.1 4.1 %multiply_reduce_fusion = (f32[128]{0:T(128)}, f32[128]{0:T(128)}, f32[128]{0:T(128)}, f32[128]{0:T(128)}, f32[128]{0:T(128)}, /*index=5*/f32[128]{0:T(128)}, f3...) fusion(f32[54,54,128]{2,1,0:T(8,128)S(1)} %maximum_convert_fusi, ...), kind=kLoop, calls=%fused_computation.161 | loop fusion | flops 12678912 | bytes 24819200 | tf_op jit(solution)/shard_map/reduce_sum | solution.py:132
  59.2 2.5 multiply_reduce_fusion.36
  61.8 3.3 %multiply_reduce_fusion.18 = (f32[128]{0:T(128)}, f32[128]{0:T(128)}, f32[128]{0:T(128)}, f32[128]{0:T(128)}, f32[128]{0:T(128)}, /*index=5*/f32[128]{0:T(128)},...) fusion(f32[48,48,128]{2,1,0:T(8,128)S(1)} %get-tuple-element.12, ...), kind=kLoop, calls=%fused_computation.179 | loop fusion | flops 10614528 | bytes 22422528 | tf_op jit(solution)/shard_map/reduce_sum | solution.py:132
  65.2 14.3 %fusion.117 = (bf16[54,54,128]{2,1,0:T(8,128)(2,1)S(1)}, f32[54,54,128]{2,1,0:T(8,128)}) fusion(f32[128]{0:T(128)} %get-tuple-element.202, f32[128]{0:T(128)} %get-tuple-element.203, f32[128]{0:T(128)S(1)} %get-tuple-element.156, f32[128]{0:T(128)S(1)} %get-tuple-element.157, f32[128]{0:T(128)S(1)} %get-tuple-element.158, f32[128]{0:T(128)S(1)} %get-tuple-element.159, ...), kind=kLoop, calls=%fused_computation.316 | loop fusion | flops 36578304 | bytes 3444224 | tf_op jit(solution)/shard_map/convert.6
  80.4 1.6 collective-permute-start.5
  82.0 1.2 fusion.126
  83.6 1.5 stack.199
  85.1 1.4 slice.989
  86.5 38.0 %psum.23 = f32[7,7,128]{2,1,0:T(8,128)S(1)} all-reduce(f32[7,7,128]{2,1,0:T(8,128)S(1)} %reshape.268), channel_id=1, replica_groups=mesh['face'=2,'tile'=16] {'face','tile'}, use_global_device_ids=true, to_apply=%region_55.56 | all-reduce | flops 6272 | bytes 50176 | tf_op jit(solution)/shard_map/psum | solution.py:230
  125.8 4.4 %collective-permute-start.7 = (bf16[48,3,128]{2,1,0:T(4,128)(2,1)S(1)}, bf16[48,3,128]{2,1,0:T(4,128)(2,1)S(1)}, u32[]{:S(2)}, u32[]{:S(2)}) collective-permute-start(bf16[48,3,128]{2,1,0:T(4,128)(2,1)S(1)} %get-tuple-element.144), channel_id=1, source_target_pairs={{1,0},{2,1},{3,2},{4,3},{5,4},{6,5},{7,6},{8,7},{9,8},{10,9},{11,1... | collective-permute-start | bytes 110600 | tf_op jit(solution)/shard_map/ppermute | solution.py:21
  131.0 1.1 collective-permute-done.6
  135.9 121.4 %all-reduce.4.cloned.1.call-done = (f32[128,512]{1,0:T(8,128)}, f32[512,128]{1,0:T(8,128)}) async-done(((f32[128,512]{1,0:T(8,128)}, f32[512,128]{1,0:T(8,128)}), (f32[128,512]{1,0:T(8,128)}, f32[512,128]{1,0:T(8,128)})) %all-reduce.4.cloned.1.call-update) | async-done | bytes 524304 | tf_op jit(solution)/shard_map/psum | solution.py:230
  257.3 1.7 broadcast_multiply_fusion.1
  259.0 1.7 broadcast_multiply_fusion
  (275 shorter events, 16.0 us)
Async XLA Ops:
  7.2 36.2 %copy-start = (bf16[128,512]{1,0:T(8,128)(2,1)S(1)}, bf16[128,512]{1,0:T(8,128)(2,1)}, u32[]{:S(2)}) copy-start(bf16[128,512]{1,0:T(8,128)(2,1)} %param.30) | copy-start | bytes 393220
  7.2 18.9 %copy-start.1 = (bf16[48,48,128]{2,1,0:T(8,128)(2,1)S(1)}, bf16[48,48,128]{2,1,0:T(8,128)(2,1)}, u32[]{:S(2)}) copy-start(bf16[48,48,128]{2,1,0:T(8,128)(2,1)} %param.24) | copy-start | bytes 1769476
  7.2 14.2 %copy-start.10 = (f32[7,7,128]{2,1,0:T(8,128)S(1)}, f32[7,7,128]{2,1,0:T(8,128)}, u32[]{:S(2)}) copy-start(f32[7,7,128]{2,1,0:T(8,128)} %param.26) | copy-start | bytes 75268
  7.2 250.1 %all-reduce.4.cloned.1.call-start = ((), (), s32[]{:S(2)}) async-start(), calls=%async_computation | async-start | bytes 1048576 | tf_op jit(solution)/shard_map/psum | solution.py:230
  15.8 10.2 %collective-permute-start = (bf16[48,3,128]{2,1,0:T(4,128)(2,1)S(1)}, bf16[48,3,128]{2,1,0:T(4,128)(2,1)S(1)}, u32[]{:S(2)}, u32[]{:S(2)}) collective-permute-start(bf16[48,3,128]{2,1,0:T(4,128)(2,1)S(1)} %get-tuple-element.145), channel_id=1, source_target_pairs={{0,1},{1,2},{2,3},{3,4},{4,5},{5,6},{6,7},{7,8},{8,9},{9,10},{10,1... | collective-permute-start | bytes 110600 | tf_op jit(solution)/shard_map/ppermute | solution.py:20
  16.4 9.7 %collective-permute-start.1 = (bf16[48,3,128]{2,1,0:T(4,128)(2,1)S(1)}, bf16[48,3,128]{2,1,0:T(4,128)(2,1)S(1)}, u32[]{:S(2)}, u32[]{:S(2)}) collective-permute-start(bf16[48,3,128]{2,1,0:T(4,128)(2,1)S(1)} %get-tuple-element.146), channel_id=1, source_target_pairs={{1,0},{2,1},{3,2},{4,3},{5,4},{6,5},{7,6},{8,7},{9,8},{10,9},{11,1... | collective-permute-start | bytes 110600 | tf_op jit(solution)/shard_map/ppermute | solution.py:21
  21.4 11.2 %copy-start.12 = (f32[128]{0:T(128)}, f32[128]{0:T(128)S(1)}, u32[]{:S(2)}) copy-start(f32[128]{0:T(128)S(1)} %get-tuple-element.168) | copy-start | bytes 1540
  21.4 11.2 %copy-start.14 = (f32[128]{0:T(128)}, f32[128]{0:T(128)S(1)}, u32[]{:S(2)}) copy-start(f32[128]{0:T(128)S(1)} %get-tuple-element.169) | copy-start | bytes 1540
  21.4 11.2 %copy-start.16 = (f32[128]{0:T(128)}, f32[128]{0:T(128)S(1)}, u32[]{:S(2)}) copy-start(f32[128]{0:T(128)S(1)} %get-tuple-element.170) | copy-start | bytes 1540
  21.4 11.2 %copy-start.18 = (f32[128]{0:T(128)}, f32[128]{0:T(128)S(1)}, u32[]{:S(2)}) copy-start(f32[128]{0:T(128)S(1)} %get-tuple-element.171) | copy-start | bytes 1540
  21.4 11.2 %copy-start.20 = (f32[128]{0:T(128)}, f32[128]{0:T(128)S(1)}, u32[]{:S(2)}) copy-start(f32[128]{0:T(128)S(1)} %get-tuple-element.172) | copy-start | bytes 1540
  21.4 11.2 %copy-start.22 = (f32[128]{0:T(128)}, f32[128]{0:T(128)S(1)}, u32[]{:S(2)}) copy-start(f32[128]{0:T(128)S(1)} %get-tuple-element.173) | copy-start | bytes 1540
  22.1 10.6 %copy-start.28 = (f32[128]{0:T(128)}, f32[128]{0:T(128)S(1)}, u32[]{:S(2)}) copy-start(f32[128]{0:T(128)S(1)} %get-tuple-element.176) | copy-start | bytes 1540
  22.1 10.6 %copy-start.30 = (f32[128]{0:T(128)}, f32[128]{0:T(128)S(1)}, u32[]{:S(2)}) copy-start(f32[128]{0:T(128)S(1)} %get-tuple-element.177) | copy-start | bytes 1540
  22.1 10.6 %copy-start.32 = (f32[128]{0:T(128)}, f32[128]{0:T(128)S(1)}, u32[]{:S(2)}) copy-start(f32[128]{0:T(128)S(1)} %get-tuple-element.178) | copy-start | bytes 1540
  22.1 10.6 %copy-start.34 = (f32[128]{0:T(128)}, f32[128]{0:T(128)S(1)}, u32[]{:S(2)}) copy-start(f32[128]{0:T(128)S(1)} %get-tuple-element.179) | copy-start | bytes 1540
  26.3 4.3 %collective-permute-start.3 = (bf16[3,54,128]{2,1,0:T(8,128)(2,1)S(1)}, bf16[3,54,128]{2,1,0:T(8,128)(2,1)S(1)}, u32[]{:S(2)}, u32[]{:S(2)}) collective-permute-start(bf16[3,54,128]{2,1,0:T(8,128)(2,1)S(1)} %broadcast_select_fusion.1), channel_id=1, source_target_pairs={{16,0},{0,16},{17,1},{1,17},{18,2},{2,18},{19,3},{3,19},{20,4},{4,... | collective-permute-start | bytes 124424 | tf_op jit(solution)/shard_map/ppermute | solution.py:21
  28.3 4.0 %collective-permute-start.2 = (bf16[3,54,128]{2,1,0:T(8,128)(2,1)S(1)}, bf16[3,54,128]{2,1,0:T(8,128)(2,1)S(1)}, u32[]{:S(2)}, u32[]{:S(2)}) collective-permute-start(bf16[3,54,128]{2,1,0:T(8,128)(2,1)S(1)} %get-tuple-element.139), channel_id=1, source_target_pairs={{0,16},{16,0},{1,17},{17,1},{2,18},{18,2},{3,19},{19,3},{4,20},{20... | collective-permute-start | bytes 124424 | tf_op jit(solution)/shard_map/ppermute | solution.py:20
  65.2 16.8 %copy-start.4 = (bf16[2304,512]{1,0:T(8,128)(2,1)S(1)}, bf16[2304,512]{1,0:T(8,128)(2,1)}, u32[]{:S(2)}) copy-start(bf16[2304,512]{1,0:T(8,128)(2,1)} %copy-done.3) | copy-start | bytes 7077892
  65.2 16.8 %copy-start.6 = (bf16[48,48,128]{2,1,0:T(8,128)(2,1)S(1)}, bf16[48,48,128]{2,1,0:T(8,128)(2,1)}, u32[]{:S(2)}) copy-start(bf16[48,48,128]{2,1,0:T(8,128)(2,1)} %copy-done.5) | copy-start | bytes 1769476
  79.5 45.0 %collective-permute-start.4 = (bf16[3,54,128]{2,1,0:T(8,128)(2,1)S(1)}, bf16[3,54,128]{2,1,0:T(8,128)(2,1)S(1)}, u32[]{:S(2)}, u32[]{:S(2)}) collective-permute-start(bf16[3,54,128]{2,1,0:T(8,128)(2,1)S(1)} %get-tuple-element.141), channel_id=1, source_target_pairs={{0,16},{16,0},{1,17},{17,1},{2,18},{18,2},{3,19},{19,3},{4,20},{20... | collective-permute-start | bytes 124424 | tf_op jit(solution)/shard_map/ppermute | solution.py:20
  80.4 44.1 %collective-permute-start.5 = (bf16[3,54,128]{2,1,0:T(8,128)(2,1)S(1)}, bf16[3,54,128]{2,1,0:T(8,128)(2,1)S(1)}, u32[]{:S(2)}, u32[]{:S(2)}) collective-permute-start(bf16[3,54,128]{2,1,0:T(8,128)(2,1)S(1)} %get-tuple-element.142), channel_id=1, source_target_pairs={{16,0},{0,16},{17,1},{1,17},{18,2},{2,18},{19,3},{3,19},{20,4},{4,... | collective-permute-start | bytes 124424 | tf_op jit(solution)/shard_map/ppermute | solution.py:21
  125.7 6.4 %collective-permute-start.6 = (bf16[48,3,128]{2,1,0:T(4,128)(2,1)S(1)}, bf16[48,3,128]{2,1,0:T(4,128)(2,1)S(1)}, u32[]{:S(2)}, u32[]{:S(2)}) collective-permute-start(bf16[48,3,128]{2,1,0:T(4,128)(2,1)S(1)} %get-tuple-element.143), channel_id=1, source_target_pairs={{0,1},{1,2},{2,3},{3,4},{4,5},{5,6},{6,7},{7,8},{8,9},{9,10},{10,1... | collective-permute-start | bytes 110600 | tf_op jit(solution)/shard_map/ppermute | solution.py:20
  125.8 6.3 %collective-permute-start.7 = (bf16[48,3,128]{2,1,0:T(4,128)(2,1)S(1)}, bf16[48,3,128]{2,1,0:T(4,128)(2,1)S(1)}, u32[]{:S(2)}, u32[]{:S(2)}) collective-permute-start(bf16[48,3,128]{2,1,0:T(4,128)(2,1)S(1)} %get-tuple-element.144), channel_id=1, source_target_pairs={{1,0},{2,1},{3,2},{4,3},{5,4},{6,5},{7,6},{8,7},{9,8},{10,9},{11,1... | collective-permute-start | bytes 110600 | tf_op jit(solution)/shard_map/ppermute | solution.py:21
  (89 other events, 271.2 us)
Sparse Core Ops, SparseCore 0:
  131.0 126.2 all-reduce.3
where the time goes:
time: 268 us; the launch traced here: 267 us
  waiting for transfers between devices  124 us (46%)
  other arithmetic  45.7 us (17%)
  blocking collectives  38 us (14%)
  between operations  24.9 us (9%)
  starting transfers between devices  14.3 us (5%)
  local copies, waits for them, and re-layouts  11.3 us (4%)
  matrix products  9.04 us (3%)
    psum x1, waiting for transfers between devices, body(): lax.psum((grad_in, grad_out, grad_kern), ('face', 'tile'))  121 us
    psum x1, blocking collectives, body(): lax.psum((grad_in, grad_out, grad_kern), ('face', 'tile'))  38 us
    another operation x2, other arithmetic  14.4 us
    ppermute x4, starting transfers between devices, extended(): after = lax.ppermute(initial, axis, down)  13.1 us
    reduce_sum x3, other arithmetic, tile_step(): jnp.sum(padded_f[row_off:row_off + tile_side, col_off:col_off + tile_side...  9.93 us
    reduce_sum x1, other arithmetic, tile_step(): center = convolved - jnp.mean(convolved, axis=-1, keepdims=True)  8.79 us
  transfers between devices with their start and end apart: 9, of which 3 were waited for; matrix products, arithmetic and copies ran while one was open for 3% of the time, Pallas kernels for 0%

commit v1 on v0

--- a/solution.py
+++ b/solution.py
@@ -1,8 +1,11 @@
+import functools
 import math
 
 import jax
 import jax.numpy as jnp
 from jax import lax
+from jax.experimental import pallas as pl
+from jax.experimental.pallas import tpu as pltpu
 from jax.sharding import PartitionSpec as P
 
 
@@ -139,6 +142,122 @@
     return (result, pad_grad, grad_in, grad_out, grad_kern)
 
 
+MESH_ID = pl.DeviceIdType.MESH
+SUB = 4
+
+
+def reduce_kernel(
+    n_face, n_tile, rows, scale, in_ref, out_ref, kern_ref, o_in, o_out, o_kern,
+    send_buf, first_buf, second_buf, all_buf, send1, recv1, send2, recv2, send3, recv3,
+):
+    face, tile = lax.axis_index("face"), lax.axis_index("tile")
+    n1, n2 = n_face * SUB, n_tile // SUB
+    me1 = face * SUB + tile % SUB
+    me2 = tile // SUB
+
+    def peer1(offset):
+        other = (me1 + offset) % n1
+        return other, (other // SUB, me2 * SUB + other % SUB)
+
+    def peer2(offset):
+        other = (me2 + offset) % n2
+        return (face, other * SUB + tile % SUB)
+
+    barrier = pltpu.get_barrier_semaphore()
+    for k in range(1, n1):
+        pl.semaphore_signal(barrier, inc=1, device_id=peer1(k)[1], device_id_type=MESH_ID)
+    for k in range(1, n2):
+        pl.semaphore_signal(barrier, inc=1, device_id=peer2(k), device_id_type=MESH_ID)
+    blocks = in_ref.shape[1] // 128
+    for q in range(blocks):
+        send_buf[q * 128 : (q + 1) * 128] = in_ref[:, q * 128 : (q + 1) * 128].astype(jnp.bfloat16)
+    base = blocks * 128
+    depth = out_ref.shape[0]
+    send_buf[base : base + depth] = out_ref[...].astype(jnp.bfloat16)
+    base2 = base + depth
+    taps = kern_ref.shape[0]
+    send_buf[base2 : base2 + taps] = kern_ref[...].astype(jnp.bfloat16)
+    if n1 * rows > base2 + taps:
+        send_buf[base2 + taps :] = jnp.zeros((n1 * rows - base2 - taps, 128), jnp.bfloat16)
+    pl.semaphore_wait(barrier, n1 + n2 - 2)
+
+    def part(index):
+        return pl.ds(pl.multiple_of(index * rows, 16), rows)
+
+    copies = []
+    for k in range(1, n1):
+        other, where = peer1(k)
+        copies.append(pltpu.make_async_remote_copy(
+            src_ref=send_buf.at[part(other)], dst_ref=first_buf.at[k - 1],
+            send_sem=send1.at[k - 1], recv_sem=recv1.at[k - 1],
+            device_id=where, device_id_type=MESH_ID))
+        copies[-1].start()
+    total = send_buf[part(me1)].astype(jnp.float32)
+    for k in range(1, n1):
+        copies[k - 1].wait_recv()
+        total = total + first_buf[k - 1].astype(jnp.float32)
+    second_buf[me2] = total.astype(jnp.bfloat16)
+    copies2 = []
+    for k in range(1, n2):
+        copies2.append(pltpu.make_async_remote_copy(
+            src_ref=second_buf.at[me2], dst_ref=second_buf.at[me2],
+            send_sem=send2.at[k - 1], recv_sem=recv2.at[k - 1],
+            device_id=peer2(k), device_id_type=MESH_ID))
+        copies2[-1].start()
+    for copy in copies2:
+        copy.wait_recv()
+    total = second_buf[0].astype(jnp.float32)
+    for k in range(1, n2):
+        total = total + second_buf[k].astype(jnp.float32)
+    all_buf[part(me1)] = total.astype(jnp.bfloat16)
+    copies3 = []
+    for k in range(1, n1):
+        copies3.append(pltpu.make_async_remote_copy(
+            src_ref=all_buf.at[part(me1)], dst_ref=all_buf.at[part(me1)],
+            send_sem=send3.at[k - 1], recv_sem=recv3.at[k - 1],
+            device_id=peer1(k)[1], device_id_type=MESH_ID))
+        copies3[-1].start()
+    for copy in copies3:
+        copy.wait_recv()
+    for copy in copies + copies2 + copies3:
+        copy.wait_send()
+    for q in range(blocks):
+        o_in[:, q * 128 : (q + 1) * 128] = all_buf[q * 128 : (q + 1) * 128].astype(jnp.float32) * scale
+    o_out[...] = all_buf[base : base + depth].astype(jnp.float32) * scale
+    o_kern[...] = all_buf[base2 : base2 + taps].astype(jnp.float32) * scale
+
+
+def reduce_sums(grad_in, grad_out, grad_kern, scale):
+    n_face, n_tile = lax.axis_size("face"), lax.axis_size("tile")
+    n1, n2 = n_face * SUB, n_tile // SUB
+    taps = -(-grad_kern.shape[0] // 16) * 16
+    kern = jnp.pad(grad_kern, ((0, taps - grad_kern.shape[0]), (0, 0)))
+    need = grad_in.shape[1] + grad_out.shape[0] + taps
+    rows = -(-need // (16 * n1)) * 16
+    vmem = pl.BlockSpec(memory_space=pltpu.VMEM)
+    bf16 = jnp.bfloat16
+    dma = pltpu.SemaphoreType.DMA
+    o_in, o_out, o_kern = pl.pallas_call(
+        functools.partial(reduce_kernel, n_face, n_tile, rows, scale),
+        out_shape=(
+            jax.ShapeDtypeStruct(grad_in.shape, jnp.float32),
+            jax.ShapeDtypeStruct(grad_out.shape, jnp.float32),
+            jax.ShapeDtypeStruct(kern.shape, jnp.float32),
+        ),
+        in_specs=[vmem] * 3,
+        out_specs=[vmem] * 3,
+        scratch_shapes=[
+            pltpu.VMEM((n1 * rows, 128), bf16),
+            pltpu.VMEM((n1 - 1, rows, 128), bf16),
+            pltpu.VMEM((n2, rows, 128), bf16),
+            pltpu.VMEM((n1 * rows, 128), bf16),
+            dma((n1 - 1,)), dma((n1 - 1,)), dma((n2 - 1,)), dma((n2 - 1,)), dma((n1 - 1,)), dma((n1 - 1,)),
+        ],
+        compiler_params=pltpu.CompilerParams(collective_id=0, has_side_effects=True, vmem_limit_bytes=32 << 20),
+    )(grad_in, grad_out, kern)
+    return o_in, o_out, o_kern[: grad_kern.shape[0]]
+
+
 def body(
     state_field,
     turn_codes,
@@ -227,17 +346,14 @@
     grad_cells = grad_cells.at[:, :margin].add(edge_grads[2])
     grad_cells = grad_cells.at[:margin].add(edge_grads[3])
     grad_field = (cotangent.astype(jnp.float32) + grad_cells).astype(jnp.bfloat16)
-    grad_in, grad_out, grad_kern = lax.psum((grad_in, grad_out, grad_kern), ("face", "tile"))
     scale_factor = 1.0 / math.sqrt(
         tile_side * tile_side * lax.axis_size("face") * lax.axis_size("tile")
     )
-    return (
-        block_out,
-        grad_field,
-        grad_in * scale_factor,
-        grad_out * scale_factor,
-        grad_kern * scale_factor,
-    )
+    taps = grad_kern.shape[0] * grad_kern.shape[1]
+    total_in, total_out, total_kern = reduce_sums(
+        grad_in, grad_out, grad_kern.reshape(taps, -1), scale_factor
+    )
+    return (block_out, grad_field, total_in, total_out, total_kern.reshape(grad_kern.shape))
 
 
 def solution(mesh):

time: 268 us -> 112 us (0.42)
  waiting for transfers between devices: 124 us -> 3.32 us
  blocking collectives: 38 us -> 0 us
  Pallas kernels: 0 us -> 15.6 us
  between operations: 24.9 us -> 12 us
  local copies, waits for them, and re-layouts: 11.3 us -> 17.9 us
  other arithmetic: 45.7 us -> 40.9 us
    psum x1 -> x0, waiting for transfers between devices: 121 us -> none  [body(): lax.psum((grad_in, grad_out, grad_kern), ('face', 'tile'))]
    psum x1 -> x0, blocking collectives: 38 us -> none  [body(): lax.psum((grad_in, grad_out, grad_kern), ('face', 'tile'))]
    pallas_call x0 -> x1, Pallas kernels: none -> 15.6 us  [reduce_sums(): pl.pallas_call(functools.partial(reduce_kernel, n_face, n_tile, rows, sca...]
    mul x3 -> x0, other arithmetic: 3.96 us -> none  [the longest x1 1.68 us: body(): grad_in * scale_factor]
    scatter-add x2, local copies, waits for them, and re-layouts: 0.66 us -> 3.36 us  [body(): grad_cells = grad_cells.at[:, tile_side - margin:].add(edge_grads[0])]
  transfers between devices with their start and end apart: 9 -> 8, of which waited for: 3 -> 3; matrix products, arithmetic and copies ran while one was open for 3% -> 5% of each run, Pallas kernels for 0% -> 14%
where the time goes in v1:
time: 112 us
  other arithmetic  40.9 us (37%)
  local copies, waits for them, and re-layouts  17.9 us (16%)
  Pallas kernels  15.6 us (14%)
  starting transfers between devices  14.2 us (13%)
  between operations  12 us (11%)
  matrix products  7.63 us (7%)
  waiting for transfers between devices  3.32 us (3%)
    pallas_call x1, Pallas kernels, reduce_sums(): pl.pallas_call(functools.partial(reduce_kernel, n_face, n_tile, rows, sca...  15.6 us
    another operation x2, other arithmetic  13.7 us
    ppermute x4, starting transfers between devices, extended(): after = lax.ppermute(initial, axis, down)  13 us
    reduce_sum x3, other arithmetic, tile_step(): jnp.sum(padded_f[row_off:row_off + tile_side, col_off:col_off + tile_side...  9.94 us
    reduce_sum x1, other arithmetic, tile_step(): center = convolved - jnp.mean(convolved, axis=-1, keepdims=True)  8.61 us
    scatter-add x2, local copies, waits for them, and re-layouts, body(): grad_cells = grad_cells.at[:, tile_side - margin:].add(edge_grads[0])  3.36 us
    unnamed x266, local copies, waits for them, and re-layouts  3.3 us
    ppermute x4, waiting for transfers between devices, extended(): before = lax.ppermute(last, axis, up)  2.84 us
  transfers between devices with their start and end apart: 8, of which 3 were waited for; matrix products, arithmetic and copies ran while one was open for 5% of the time, Pallas kernels for 14%

profile of v1, /device:TPU:0, one launch (start us, length us, event | category | flops | bytes accessed | tf_op | source)
XLA Modules:
  0.0 111.6 jit_solution(12528066033835603178)
XLA Ops:
  0.7 1.4 %fusion.125 = (s32[1,1,1]{2,1,0:T(1,128)}, s32[1,1,1]{2,1,0:T(1,128)}, s32[1,1,1]{2,1,0:T(1,128)}, s32[1,1,1]{2,1,0:T(1,128)}) fusion(s32[1,1,4]{2,1,0:T(1,128)} %param.25), kind=kLoop, calls=%fused_computation.320 | loop fusion | bytes 32 | tf_op jit(solution)/shard_map/slice | solution.py:285
  6.7 1.0 fusion.122
  8.2 1.1 fusion.114
  9.8 5.0 %collective-permute-start.1 = (bf16[48,3,128]{2,1,0:T(4,128)(2,1)S(1)}, bf16[48,3,128]{2,1,0:T(4,128)(2,1)S(1)}, u32[]{:S(2)}, u32[]{:S(2)}) collective-permute-start(bf16[48,3,128]{2,1,0:T(4,128)(2,1)S(1)} %get-tuple-element.150), channel_id=1, source_target_pairs={{1,0},{2,1},{3,2},{4,3},{5,4},{6,5},{7,6},{8,7},{9,8},{10,9},{11,1... | collective-permute-start | bytes 110600 | tf_op jit(solution)/shard_map/ppermute | solution.py:24
  19.7 2.0 %collective-permute-start.3 = (bf16[3,54,128]{2,1,0:T(8,128)(2,1)S(1)}, bf16[3,54,128]{2,1,0:T(8,128)(2,1)S(1)}, u32[]{:S(2)}, u32[]{:S(2)}) collective-permute-start(bf16[3,54,128]{2,1,0:T(8,128)(2,1)S(1)} %broadcast_select_fusion.1), channel_id=1, source_target_pairs={{16,0},{0,16},{17,1},{1,17},{18,2},{2,18},{19,3},{3,19},{20,4},{4,... | collective-permute-start | bytes 124424 | tf_op jit(solution)/shard_map/ppermute | solution.py:24
  24.0 1.8 %collective-permute-done.2 = bf16[3,54,128]{2,1,0:T(8,128)(2,1)S(1)} collective-permute-done((bf16[3,54,128]{2,1,0:T(8,128)(2,1)S(1)}, bf16[3,54,128]{2,1,0:T(8,128)(2,1)S(1)}, u32[]{:S(2)}, u32[]{:S(2)}) %collective-permute-start.2) | collective-permute-done | bytes 41504 | tf_op jit(solution)/shard_map/ppermute | solution.py:23
  26.4 8.6 %fusion.119 = (f32[48,48]{1,0:T(8,128)S(1)}, f32[48,48,128]{2,1,0:T(8,128)S(1)}) fusion(f32[128]{0:T(128)S(1)} %copy-done.131, f32[128]{0:T(128)S(1)} %copy-done.85, f32[54,54,128]{2,1,0:T(8,128)S(1)} %maximum_convert_fusion, f32[128]{0:T(128)S(1)} %copy-done.87, f32[128]{0:T(128)S(1)} %get-tuple-element.160, f32[128]{0:T(128)S(1)} %get-tuple-element.161, ...), kind=kLoop, calls=%fused_computation.314 | loop fusion | flops 29193984 | bytes 59017216 | tf_op jit(solution)/shard_map/reduce_sum | solution.py:91
  36.6 1.5 %multiply_convert_fusion = (bf16[2304,512]{1,0:T(8,128)(2,1)S(1)}, f32[2304,512]{1,0:T(8,128)S(1)}) fusion(f32[512]{0:T(512)S(1)} %copy-done.89, bf16[2304,128]{1,0:T(8,128)(2,1)S(1)} %bitcast.205, bf16[128,512]{1,0:T(8,128)(2,1)S(1)} %copy-done), kind=kOutput, calls=%fused_computation.56 | convolution fusion | flops 309067776 | bytes 7800832 | tf_op jit(solution)/shard_map/dot_general | solution.py:95
  39.7 1.1 %fusion.102 = (bf16[48,48,128]{2,1,0:T(8,128)(2,1)S(1)}, bf16[48,48,128]{2,1,0:T(8,128)(2,1)}) fusion(bf16[48,48,128]{2,1,0:T(8,128)(2,1)S(1)} %copy-done.10, f32[128]{0:T(128)S(1)} %copy-done.130, f32[48,48,128]{2,1,0:T(8,128)S(1)} %bitcast.204, bf16[48,48,128]{2,1,0:T(8,128)(2,1)S(1)} %copy-done.3), kind=kLoop, calls=%fused_computation.159 | loop fusion | flops 2064384 | bytes 3539456 | tf_op jit(solution)/shard_map/convert_element_type | solution.py:104
  40.8 2.2 %fusion.4 = bf16[2304,512]{1,0:T(8,128)(2,1)S(1)} fusion(f32[2304,512]{1,0:T(8,128)S(1)} %get-tuple-element.215, bf16[2304,128]{1,0:T(8,128)(2,1)S(1)} %bitcast.207, bf16[512,128]{1,0:T(8,128)(2,1)S(1)} %copy-done.14), kind=kOutput, calls=%fused_computation.58 | convolution fusion | flops 313786368 | bytes 7798784 | tf_op jit(solution)/shard_map/dot_general | solution.py:107
  43.1 1.8 %multiply_reduce_fusion.50 = (f32[2304]{0:T(1024)S(1)}, f32[2304,128]{1,0:T(8,128)}) fusion(f32[128]{0:T(128)S(1)} %copy-done.16, bf16[2304,512]{1,0:T(8,128)(2,1)S(1)} %fusion.4, bf16[128,512]{1,0:T(8,128)(2,1)S(1)} %copy-done), kind=kOutput, calls=%fused_computation.212 | convolution fusion | flops 302577408 | bytes 3679744 | tf_op jit(solution)/shard_map/dot_general | solution.py:111
  45.0 2.3 %multiply_reduce_fusion.49 = f32[48,48]{1,0:T(8,128)S(1)} fusion(f32[48,48,128]{2,1,0:T(8,128)} %bitcast.202, f32[48,48,128]{2,1,0:T(8,128)S(1)} %get-tuple-element.142, f32[128]{0:T(128)S(1)} %copy-done.16, f32[48,48]{1,0:T(8,128)S(1)} %add_rsqrt_fusion, f32[48,48]{1,0:T(8,128)S(1)} %broadcast_multiply_fusion.1), kind=kLoop, calls=%fused_computation.211 | loop fusion | flops 1472256 | bytes 2387456 | tf_op jit(solution)/shard_map/reduce_sum | solution.py:117
  47.3 4.1 %multiply_reduce_fusion = (f32[128]{0:T(128)}, f32[128]{0:T(128)}, f32[128]{0:T(128)}, f32[128]{0:T(128)}, f32[128]{0:T(128)}, /*index=5*/f32[128]{0:T(128)}, f3...) fusion(f32[54,54,128]{2,1,0:T(8,128)S(1)} %maximum_convert_fusi, ...), kind=kLoop, calls=%fused_computation.161 | loop fusion | flops 12678912 | bytes 24819200 | tf_op jit(solution)/shard_map/reduce_sum | solution.py:135
  51.4 2.5 %multiply_reduce_fusion.36 = (f32[128]{0:T(128)}, f32[128]{0:T(128)}, f32[128]{0:T(128)}, f32[128]{0:T(128)}, f32[128]{0:T(128)}, /*index=5*/f32[128]{0:T(128)},...) fusion(f32[48,48,128]{2,1,0:T(8,128)S(1)} %get-tuple-element.13, ...), kind=kLoop, calls=%fused_computation.197 | loop fusion | flops 7666048 | bytes 16521728 | tf_op jit(solution)/shard_map/reduce_sum | solution.py:135
  54.2 3.3 %multiply_reduce_fusion.18 = (f32[128]{0:T(128)}, f32[128]{0:T(128)}, f32[128]{0:T(128)}, f32[128]{0:T(128)}, f32[128]{0:T(128)}, /*index=5*/f32[128]{0:T(128)},...) fusion(f32[48,48,128]{2,1,0:T(8,128)S(1)} %get-tuple-element.13, ...), kind=kLoop, calls=%fused_computation.179 | loop fusion | flops 10614528 | bytes 22422528 | tf_op jit(solution)/shard_map/reduce_sum | solution.py:135
  57.9 13.6 %fusion.117 = (bf16[54,54,128]{2,1,0:T(8,128)(2,1)}, f32[54,54,128]{2,1,0:T(8,128)}) fusion(f32[128]{0:T(128)S(1)} %copy-done.86, f32[128]{0:T(128)S(1)} %copy-done.88, f32[128]{0:T(128)S(1)} %get-tuple-element.160, f32[128]{0:T(128)S(1)} %get-tuple-element.161, f32[128]{0:T(128)S(1)} %get-tuple-element.162, f32[128]{0:T(128)S(1)} %get-tuple-element.163, ...), kind=kLoop, calls=%fused_computation.313 | loop fusion | flops 36578304 | bytes 3444224 | tf_op jit(solution)/shard_map/convert.6
  72.8 1.6 %collective-permute-start.5 = (bf16[3,54,128]{2,1,0:T(8,128)(2,1)S(1)}, bf16[3,54,128]{2,1,0:T(8,128)(2,1)S(1)}, u32[]{:S(2)}, u32[]{:S(2)}) collective-permute-start(bf16[3,54,128]{2,1,0:T(8,128)(2,1)S(1)} %get-tuple-element.146), channel_id=1, source_target_pairs={{16,0},{0,16},{17,1},{1,17},{18,2},{2,18},{19,3},{3,19},{20,4},{4,... | collective-permute-start | bytes 124424 | tf_op jit(solution)/shard_map/ppermute | solution.py:24
  75.3 1.1 collective-permute-done.4
  78.6 4.5 %collective-permute-start.7 = (bf16[48,3,128]{2,1,0:T(4,128)(2,1)S(1)}, bf16[48,3,128]{2,1,0:T(4,128)(2,1)S(1)}, u32[]{:S(2)}, u32[]{:S(2)}) collective-permute-start(bf16[48,3,128]{2,1,0:T(4,128)(2,1)S(1)} %get-tuple-element.148), channel_id=1, source_target_pairs={{1,0},{2,1},{3,2},{4,3},{5,4},{6,5},{7,6},{8,7},{9,8},{10,9},{11,1... | collective-permute-start | bytes 110600 | tf_op jit(solution)/shard_map/ppermute | solution.py:24
  83.9 1.5 %stack.199 = f32[49,128]{1,0:T(8,128)S(1)} concatenate(f32[1,128]{1,0:T(1,128)S(1)} %bitcast.240, f32[1,128]{1,0:T(1,128)S(1)} %bitcast.239, f32[1,128]{1,0:T(1,128)S(1)} %bitcast.238, f32[1,128]{1,0:T(1,128)S(1)} %bitcast.237, f32[1,128]{1,0:T(1,128)S(1)} %bitcast.236, f32[1,128]{1,0:T(1,128)S(1)} %bitcast.235, f32[1,128]{1,0:T(1,128)S(1)} %bitcast.234, f32[1,128]{1,0:T(1,128)S(1)} %bitcast.233, ...), dimensions={0} | concatenate | bytes 50176 | tf_op jit(solution)/shard_map/stack | solution.py:141
  85.4 15.6 %shard_map.155 = (f32[128,512]{1,0:T(8,128)S(1)}, f32[512,128]{1,0:T(8,128)S(1)}, f32[64,128]{1,0:T(8,128)S(1)}) custom-call(f32[128,512]{1,0:T(8,128)S(1)} %fusion.126.in_ref, f32[512,128]{1,0:T(8,128)S(1)} %fusion.127.out_ref, f32[64,128]{1,0:T(8,128)S(1)} %pad.21.kern_ref), custom_call_target="tpu_custom_call" | custom-call | tf_op jit(solution)/shard_map/pallas_call | solution.py:240
  101.7 1.1 slice.998
  103.5 1.7 %scatter-add.24 = f32[48,48,128]{2,1,0:T(8,128)} dynamic-update-slice(f32[48,48,128]{2,1,0:T(8,128)} %slice.998, f32[48,3,128]{2,1,0:T(4,128)S(1)} %slice_add_fusion, s32[]{:T(128)} %constant.191.clone.1, s32[]{:T(128)} %constant.205.clone.1, s32[]{:T(128)} %constant.191.clone.1) | dynamic-update-slice | bytes 147460 | tf_op jit(solution)/shard_map/scatter-add | solution.py:344
  106.1 1.7 %copy.23 = f32[48,48,128]{2,0,1:T(8,128)S(1)} copy(f32[48,48,128]{2,1,0:T(8,128)} %scatter-add.24) | data formatting | bytes 2359296 | tf_op jit(solution)/shard_map/scatter-add | solution.py:344
  (329 shorter events, 17.6 us)
Async XLA Ops:
  0.6 35.9 %copy-start = (bf16[128,512]{1,0:T(8,128)(2,1)S(1)}, bf16[128,512]{1,0:T(8,128)(2,1)}, u32[]{:S(2)}) copy-start(bf16[128,512]{1,0:T(8,128)(2,1)} %param.30) | copy-start | bytes 393220
  0.6 18.9 %copy-start.3 = (bf16[48,48,128]{2,1,0:T(8,128)(2,1)S(1)}, bf16[48,48,128]{2,1,0:T(8,128)(2,1)}, u32[]{:S(2)}) copy-start(bf16[48,48,128]{2,1,0:T(8,128)(2,1)} %param.24) | copy-start | bytes 1769476
  0.7 14.1 %copy-start.15 = (f32[7,7,128]{2,1,0:T(8,128)S(1)}, f32[7,7,128]{2,1,0:T(8,128)}, u32[]{:S(2)}) copy-start(f32[7,7,128]{2,1,0:T(8,128)} %param.26) | copy-start | bytes 75268
  9.3 10.2 %collective-permute-start = (bf16[48,3,128]{2,1,0:T(4,128)(2,1)S(1)}, bf16[48,3,128]{2,1,0:T(4,128)(2,1)S(1)}, u32[]{:S(2)}, u32[]{:S(2)}) collective-permute-start(bf16[48,3,128]{2,1,0:T(4,128)(2,1)S(1)} %get-tuple-element.149), channel_id=1, source_target_pairs={{0,1},{1,2},{2,3},{3,4},{4,5},{5,6},{6,7},{7,8},{8,9},{9,10},{10,1... | collective-permute-start | bytes 110600 | tf_op jit(solution)/shard_map/ppermute | solution.py:23
  9.8 9.7 %collective-permute-start.1 = (bf16[48,3,128]{2,1,0:T(4,128)(2,1)S(1)}, bf16[48,3,128]{2,1,0:T(4,128)(2,1)S(1)}, u32[]{:S(2)}, u32[]{:S(2)}) collective-permute-start(bf16[48,3,128]{2,1,0:T(4,128)(2,1)S(1)} %get-tuple-element.150), channel_id=1, source_target_pairs={{1,0},{2,1},{3,2},{4,3},{5,4},{6,5},{7,6},{8,7},{9,8},{10,9},{11,1... | collective-permute-start | bytes 110600 | tf_op jit(solution)/shard_map/ppermute | solution.py:24
  14.8 11.2 %copy-start.17 = (f32[128]{0:T(128)}, f32[128]{0:T(128)S(1)}, u32[]{:S(2)}) copy-start(f32[128]{0:T(128)S(1)} %get-tuple-element.172) | copy-start | bytes 1540
  14.8 11.2 %copy-start.19 = (f32[128]{0:T(128)}, f32[128]{0:T(128)S(1)}, u32[]{:S(2)}) copy-start(f32[128]{0:T(128)S(1)} %get-tuple-element.173) | copy-start | bytes 1540
  14.8 11.2 %copy-start.21 = (f32[128]{0:T(128)}, f32[128]{0:T(128)S(1)}, u32[]{:S(2)}) copy-start(f32[128]{0:T(128)S(1)} %get-tuple-element.174) | copy-start | bytes 1540
  14.8 11.2 %copy-start.23 = (f32[128]{0:T(128)}, f32[128]{0:T(128)S(1)}, u32[]{:S(2)}) copy-start(f32[128]{0:T(128)S(1)} %get-tuple-element.175) | copy-start | bytes 1540
  14.9 11.2 %copy-start.25 = (f32[128]{0:T(128)}, f32[128]{0:T(128)S(1)}, u32[]{:S(2)}) copy-start(f32[128]{0:T(128)S(1)} %get-tuple-element.176) | copy-start | bytes 1540
  14.9 11.2 %copy-start.27 = (f32[128]{0:T(128)}, f32[128]{0:T(128)S(1)}, u32[]{:S(2)}) copy-start(f32[128]{0:T(128)S(1)} %get-tuple-element.177) | copy-start | bytes 1540
  15.5 10.6 %copy-start.31 = (f32[128]{0:T(128)}, f32[128]{0:T(128)S(1)}, u32[]{:S(2)}) copy-start(f32[128]{0:T(128)S(1)} %get-tuple-element.179) | copy-start | bytes 1540
  15.5 10.6 %copy-start.33 = (f32[128]{0:T(128)}, f32[128]{0:T(128)S(1)}, u32[]{:S(2)}) copy-start(f32[128]{0:T(128)S(1)} %get-tuple-element.180) | copy-start | bytes 1540
  15.5 10.6 %copy-start.35 = (f32[128]{0:T(128)}, f32[128]{0:T(128)S(1)}, u32[]{:S(2)}) copy-start(f32[128]{0:T(128)S(1)} %get-tuple-element.181) | copy-start | bytes 1540
  15.5 10.6 %copy-start.37 = (f32[128]{0:T(128)}, f32[128]{0:T(128)S(1)}, u32[]{:S(2)}) copy-start(f32[128]{0:T(128)S(1)} %get-tuple-element.182) | copy-start | bytes 1540
  15.6 10.6 %copy-start.39 = (f32[128]{0:T(128)}, f32[128]{0:T(128)S(1)}, u32[]{:S(2)}) copy-start(f32[128]{0:T(128)S(1)} %get-tuple-element.183) | copy-start | bytes 1540
  19.7 4.2 %collective-permute-start.3 = (bf16[3,54,128]{2,1,0:T(8,128)(2,1)S(1)}, bf16[3,54,128]{2,1,0:T(8,128)(2,1)S(1)}, u32[]{:S(2)}, u32[]{:S(2)}) collective-permute-start(bf16[3,54,128]{2,1,0:T(8,128)(2,1)S(1)} %broadcast_select_fusion.1), channel_id=1, source_target_pairs={{16,0},{0,16},{17,1},{1,17},{18,2},{2,18},{19,3},{3,19},{20,4},{4,... | collective-permute-start | bytes 124424 | tf_op jit(solution)/shard_map/ppermute | solution.py:24
  21.7 4.0 %collective-permute-start.2 = (bf16[3,54,128]{2,1,0:T(8,128)(2,1)S(1)}, bf16[3,54,128]{2,1,0:T(8,128)(2,1)S(1)}, u32[]{:S(2)}, u32[]{:S(2)}) collective-permute-start(bf16[3,54,128]{2,1,0:T(8,128)(2,1)S(1)} %get-tuple-element.143), channel_id=1, source_target_pairs={{0,16},{16,0},{1,17},{17,1},{2,18},{18,2},{3,19},{19,3},{4,20},{20... | collective-permute-start | bytes 124424 | tf_op jit(solution)/shard_map/ppermute | solution.py:23
  57.9 16.5 %copy-start.2 = (bf16[2304,512]{1,0:T(8,128)(2,1)S(1)}, bf16[2304,512]{1,0:T(8,128)(2,1)}, u32[]{:S(2)}) copy-start(bf16[2304,512]{1,0:T(8,128)(2,1)} %copy-done.1) | copy-start | bytes 7077892
  57.9 16.5 %copy-start.13 = (bf16[48,48,128]{2,1,0:T(8,128)(2,1)S(1)}, bf16[48,48,128]{2,1,0:T(8,128)(2,1)}, u32[]{:S(2)}) copy-start(bf16[48,48,128]{2,1,0:T(8,128)(2,1)} %copy-done.12) | copy-start | bytes 1769476
  72.3 4.1 %collective-permute-start.4 = (bf16[3,54,128]{2,1,0:T(8,128)(2,1)S(1)}, bf16[3,54,128]{2,1,0:T(8,128)(2,1)S(1)}, u32[]{:S(2)}, u32[]{:S(2)}) collective-permute-start(bf16[3,54,128]{2,1,0:T(8,128)(2,1)S(1)} %get-tuple-element.145), channel_id=1, source_target_pairs={{0,16},{16,0},{1,17},{17,1},{2,18},{18,2},{3,19},{19,3},{4,20},{20... | collective-permute-start | bytes 124424 | tf_op jit(solution)/shard_map/ppermute | solution.py:23
  72.8 4.0 %collective-permute-start.5 = (bf16[3,54,128]{2,1,0:T(8,128)(2,1)S(1)}, bf16[3,54,128]{2,1,0:T(8,128)(2,1)S(1)}, u32[]{:S(2)}, u32[]{:S(2)}) collective-permute-start(bf16[3,54,128]{2,1,0:T(8,128)(2,1)S(1)} %get-tuple-element.146), channel_id=1, source_target_pairs={{16,0},{0,16},{17,1},{1,17},{18,2},{2,18},{19,3},{3,19},{20,4},{4,... | collective-permute-start | bytes 124424 | tf_op jit(solution)/shard_map/ppermute | solution.py:24
  78.1 24.7 %collective-permute-start.6 = (bf16[48,3,128]{2,1,0:T(4,128)(2,1)S(1)}, bf16[48,3,128]{2,1,0:T(4,128)(2,1)S(1)}, u32[]{:S(2)}, u32[]{:S(2)}) collective-permute-start(bf16[48,3,128]{2,1,0:T(4,128)(2,1)S(1)} %get-tuple-element.147), channel_id=1, source_target_pairs={{0,1},{1,2},{2,3},{3,4},{4,5},{5,6},{6,7},{7,8},{8,9},{9,10},{10,1... | collective-permute-start | bytes 110600 | tf_op jit(solution)/shard_map/ppermute | solution.py:23
  78.6 24.2 %collective-permute-start.7 = (bf16[48,3,128]{2,1,0:T(4,128)(2,1)S(1)}, bf16[48,3,128]{2,1,0:T(4,128)(2,1)S(1)}, u32[]{:S(2)}, u32[]{:S(2)}) collective-permute-start(bf16[48,3,128]{2,1,0:T(4,128)(2,1)S(1)} %get-tuple-element.148), channel_id=1, source_target_pairs={{1,0},{2,1},{3,2},{4,3},{5,4},{6,5},{7,6},{8,7},{9,8},{10,9},{11,1... | collective-permute-start | bytes 110600 | tf_op jit(solution)/shard_map/ppermute | solution.py:24
  (116 other events, 448.1 us)

commit v2 on v0

v2 whole, which is shorter than its diff:
```python
import functools
import math

import jax
import jax.numpy as jnp
from jax import lax
from jax.experimental import pallas as pl
from jax.experimental.pallas import tpu as pltpu
from jax.sharding import PartitionSpec as P

MESH_ID = pl.DeviceIdType.MESH
SUB = 4
F32 = jnp.float32
BF16 = jnp.bfloat16


def block_kernel(
    n_face, n_tile, rows, scale, side, ks,
    codes, x_ref, cot_ref, dk_ref, cb_ref, gain_ref, shift_ref, win_ref, bin_ref, wout_ref, bout_ref, ls_ref,
    out_ref, gf_ref, o_in, o_out, o_kern,
    xpad, xs, gs, pg, kacc, acc_in, acc_out,
    col_send, col_recv, row_send, row_recv, grow_send, grow_recv, gcol_send, gcol_recv,
    send_buf, first_buf, second_buf, all_buf,
    halo_s, halo_r, send1, recv1, send2, recv2, send3, recv3,
):
    m = ks // 2
    S = side
    wide = S + 2 * m
    C = x_ref.shape[2]
    face, tile = lax.axis_index("face"), lax.axis_index("tile")
    n1, n2 = n_face * SUB, n_tile // SUB
    me1 = face * SUB + tile % SUB
    me2 = tile // SUB
    east, west = (face, (tile + 1) % n_tile), (face, (tile + n_tile - 1) % n_tile)
    below, above = ((face + 1) % n_face, tile), ((face + n_face - 1) % n_face, tile)

    def peer1(offset):
        other = (me1 + offset) % n1
        return other, (other // SUB, me2 * SUB + other % SUB)

    def peer2(offset):
        return (face, ((me2 + offset) % n2) * SUB + tile % SUB)

    barrier = pltpu.get_barrier_semaphore()
    for where in (east, west, below, above):
        pl.semaphore_signal(barrier, inc=1, device_id=where, device_id_type=MESH_ID)
    for k in range(1, n1):
        pl.semaphore_signal(barrier, inc=1, device_id=peer1(k)[1], device_id_type=MESH_ID)
    for k in range(1, n2):
        pl.semaphore_signal(barrier, inc=1, device_id=peer2(k), device_id_type=MESH_ID)

    def remote(src, dst, sems, index, where):
        copy = pltpu.make_async_remote_copy(
            src_ref=src, dst_ref=dst, send_sem=sems[0].at[index], recv_sem=sems[1].at[index],
            device_id=where, device_id_type=MESH_ID)
        copy.start()
        return copy

    halo = (halo_s, halo_r)
    q = [codes[i] for i in range(4)]

    def mirror(n, k, total):
        r = lax.broadcasted_iota(jnp.int32, (n, k), 0)
        c = lax.broadcasted_iota(jnp.int32, (n, k), 1)
        return jnp.where(r + c == total, 1.0, 0.0).astype(BF16)

    def flip(perm, value):
        return jnp.dot(perm, value.astype(BF16), preferred_element_type=F32)

    edge = jnp.zeros((wide, 8, C), F32)
    xpad[:, 0:8] = edge
    xpad[:, S + 8 : S + 16] = edge

    @pl.loop(0, S // 8)
    def _(i):
        xpad[pl.ds(m + i * 8, 8), 8 : 8 + S] = x_ref[pl.ds(i * 8, 8)].astype(F32)

    perm_s = mirror(S, S, S - 1)

    def col(j):
        return xpad[m : m + S, 8 + j, :]

    def row(j):
        return xpad[m + j, 8 : 8 + S, :]

    def turned(code, options):
        src = jnp.where(code == 1, options[1], options[0])
        src = jnp.where(code == 2, options[2], src)
        src = jnp.where(code == 3, options[3], src)
        return jnp.where((code == 1) | (code == 2), flip(perm_s, src), src)

    cols = {j: col(j) for j in list(range(m)) + list(range(S - m, S))}
    lines = {j: row(j) for j in list(range(m)) + list(range(S - m, S))}
    for j in range(m):
        hi, lo, opp = S - m + j, m - 1 - j, S - 1 - j
        col_send[0, j] = turned(q[0], [cols[hi], lines[hi], cols[lo], lines[lo]]).astype(BF16)
        col_send[1, j] = turned(q[1], [cols[j], lines[j], cols[opp], lines[opp]]).astype(BF16)
    pl.semaphore_wait(barrier, n1 + n2 + 2)
    halo_copies = [
        remote(col_send.at[0], col_recv.at[0], halo, 0, east),
        remote(col_send.at[1], col_recv.at[1], halo, 1, west),
    ]

    rim = gs.shape[2]

    @pl.loop(0, ks)
    def _(b):
        gs[b, 0 : 2 * m] = jnp.zeros((2 * m, rim, C), F32)
        gs[b, S + 2 * m :] = jnp.zeros((2 * m, rim, C), F32)

        @pl.loop(0, S // 8)
        def _(i):
            gs[b, pl.ds(2 * m + i * 8, 8), 0:8] = jnp.zeros((8, 8, C), F32)
            gs[b, pl.ds(2 * m + i * 8, 8), S : S + 8] = jnp.zeros((8, 8, C), F32)

    kacc[...] = jnp.zeros(kacc.shape, F32)
    acc_in[...] = jnp.zeros(acc_in.shape, F32)
    acc_out[...] = jnp.zeros(acc_out.shape, F32)

    def shifted(first, count):
        for b in range(ks):
            xs[b, pl.ds(first, count)] = xpad[pl.ds(first, count), 8 - m + b : 8 - m + b + S]

    halo_copies[0].wait_recv()
    halo_copies[1].wait_recv()
    for j in range(m):
        xpad[m : m + S, 8 - m + j, :] = col_recv[0, j].astype(F32)
        xpad[m : m + S, 8 + S + j, :] = col_recv[1, j].astype(F32)
    perm_w = mirror(S + 16, S + 16, S + 15)
    for i in range(m):
        south = jnp.where(q[2] % 2 == 0, xpad[S + i], flip(perm_w, xpad[2 * m - 1 - i]))
        north = jnp.where(q[3] % 2 == 0, xpad[m + i], flip(perm_w, xpad[m + S - 1 - i]))
        row_send[0, i] = south.astype(BF16)
        row_send[1, i] = north.astype(BF16)
    halo_copies += [
        remote(row_send.at[0], row_recv.at[0], halo, 2, below),
        remote(row_send.at[1], row_recv.at[1], halo, 3, above),
    ]

    @pl.loop(0, S // 6)
    def _(i):
        shifted(m + i * 6, 6)

    halo_copies[2].wait_recv()
    halo_copies[3].wait_recv()
    xpad[0:m] = row_recv[0].astype(F32)
    xpad[m + S :] = row_recv[1].astype(F32)
    shifted(0, m)
    shifted(m + S, m)

    R = 8
    M = R * S
    contract0 = (((0,), (0,)), ((), ()))
    contract1 = (((1,), (1,)), ((), ()))

    @pl.loop(0, S // R)
    def _(i):
        i0 = i * R
        parts = []
        for s in range(0, R, 4):
            acc = jnp.zeros((4, S, C), F32)
            for a in range(ks):
                for b in range(ks):
                    acc = acc + xs[b, pl.ds(i0 + s + a, 4)] * dk_ref[a * ks + b : a * ks + b + 1]
            parts.append(acc.reshape(4 * S, C))
        conv = jnp.concatenate(parts, axis=0) + cb_ref[...]
        center = conv - jnp.mean(conv, axis=-1, keepdims=True)
        inverse = lax.rsqrt(jnp.mean(center * center, axis=-1, keepdims=True) + 1e-06)
        normed = center * inverse
        gain = gain_ref[...]
        norm_rows = (normed * gain + shift_ref[...]).astype(BF16)
        hidden = jnp.dot(norm_rows, win_ref[...], preferred_element_type=F32) + bin_ref[...]
        cdf = 0.5 * (1.0 + lax.erf(hidden * 0.7071067811865476))
        pdf = jnp.exp(-0.5 * hidden * hidden) * 0.3989422804014327
        active = (hidden * cdf).astype(BF16)
        mixed = jnp.dot(active, wout_ref[...], preferred_element_type=F32) + bout_ref[...]
        tile_in = x_ref[pl.ds(i0, R)].astype(F32).reshape(M, C)
        out_ref[pl.ds(i0, R)] = (tile_in + ls_ref[...] * mixed).astype(BF16).reshape(R, S, C)
        cot = cot_ref[pl.ds(i0, R)].astype(F32).reshape(M, C)
        grad_mixed = (cot * ls_ref[...]).astype(BF16)
        acc_out[...] += lax.dot_general(grad_mixed, active, contract0, preferred_element_type=F32)
        grad_active = lax.dot_general(grad_mixed, wout_ref[...], contract1, preferred_element_type=F32)
        grad_hidden = (grad_active * (cdf + hidden * pdf)).astype(BF16)
        acc_in[...] += lax.dot_general(norm_rows, grad_hidden, contract0, preferred_element_type=F32)
        gn = lax.dot_general(grad_hidden, win_ref[...], contract1, preferred_element_type=F32) * gain
        g = inverse * (
            gn - jnp.mean(gn, axis=-1, keepdims=True)
            - normed * jnp.mean(gn * normed, axis=-1, keepdims=True)
        )
        g = g.reshape(R, S, C)
        for b in range(ks):
            gs[b, pl.ds(i0 + 2 * m, R), b : b + S] = g

    def spread(p):
        acc = jnp.zeros((m, rim, C), F32)
        for a in range(ks):
            for b in range(ks):
                acc = acc + gs[b, pl.ds(p + 2 * m - a, m)] * dk_ref[a * ks + b : a * ks + b + 1]
        pg[pl.ds(p, m)] = acc

    @pl.loop(0, 2)
    def _(e):
        spread(e * (S + m))

    gap = jnp.zeros((m, 64 - rim, C), F32)
    grow_send[0] = jnp.concatenate([pg[0:m], gap], axis=1).astype(BF16)
    grow_send[1] = jnp.concatenate([pg[S + m :], gap], axis=1).astype(BF16)
    halo_copies += [
        remote(grow_send.at[0], grow_recv.at[0], halo, 4, above),
        remote(grow_send.at[1], grow_recv.at[1], halo, 5, below),
    ]

    @pl.loop(0, S // 4)
    def _(i):
        g = gs[0, pl.ds(i * 4 + 2 * m, 4), 0:S]
        for a in range(ks):
            for b in range(ks):
                prod = xs[b, pl.ds(i * 4 + a, 4)] * g
                kacc[a * ks + b] += jnp.sum(prod.reshape(S // 2, 8, C), axis=0)

    blocks = acc_in.shape[1] // 128
    base = blocks * 128
    for k in range(blocks):
        send_buf[k * 128 : (k + 1) * 128] = acc_in[:, k * 128 : (k + 1) * 128].astype(BF16)
        send_buf[base + k * 128 : base + (k + 1) * 128] = acc_out[:, k * 128 : (k + 1) * 128].T.astype(BF16)
    taps = kacc.shape[0]
    send_buf[2 * base : 2 * base + taps] = jnp.sum(kacc[...], axis=1).astype(BF16)
    if n1 * rows > 2 * base + taps:
        send_buf[2 * base + taps :] = jnp.zeros((n1 * rows - 2 * base - taps, 128), BF16)

    def part(index):
        return pl.ds(pl.multiple_of(index * rows, 16), rows)

    copies = []
    for k in range(1, n1):
        other, where = peer1(k)
        copies.append(remote(send_buf.at[part(other)], first_buf.at[k - 1], (send1, recv1), k - 1, where))

    third = S // m // 2

    @pl.loop(0, third)
    def _(i):
        spread(m + i * m)

    total = send_buf[part(me1)].astype(F32)
    for k in range(1, n1):
        copies[k - 1].wait_recv()
        total = total + first_buf[k - 1].astype(F32)
    second_buf[me2] = total.astype(BF16)
    copies2 = []
    for k in range(1, n2):
        copies2.append(remote(second_buf.at[me2], second_buf.at[me2], (send2, recv2), k - 1, peer2(k)))

    @pl.loop(third, S // m)
    def _(i):
        spread(m + i * m)

    halo_copies[4].wait_recv()
    halo_copies[5].wait_recv()
    perm_r = mirror(rim, 64, wide - 1)
    for i in range(m):
        top_turned = flip(perm_r, grow_recv[0, m - 1 - i])
        end_turned = flip(perm_r, grow_recv[1, m - 1 - i])
        north = grow_recv[1, i].astype(F32)[:rim]
        south = grow_recv[0, i].astype(F32)[:rim]
        pg[m + i] += jnp.where(q[3] % 2 == 0, north, 0.0) + jnp.where(q[2] % 2 == 1, top_turned, 0.0)
        pg[S + i] += jnp.where(q[3] % 2 == 1, end_turned, 0.0) + jnp.where(q[2] % 2 == 0, south, 0.0)
    for j in range(m):
        gcol_send[0, j] = pg[m : m + S, j, :].astype(BF16)
        gcol_send[1, j] = pg[m : m + S, S + m + j, :].astype(BF16)
    halo_copies += [
        remote(gcol_send.at[0], gcol_recv.at[0], halo, 6, west),
        remote(gcol_send.at[1], gcol_recv.at[1], halo, 7, east),
    ]

    for copy in copies2:
        copy.wait_recv()
    total = second_buf[0].astype(F32)
    for k in range(1, n2):
        total = total + second_buf[k].astype(F32)
    all_buf[part(me1)] = total.astype(BF16)
    copies3 = []
    for k in range(1, n1):
        copies3.append(
            remote(all_buf.at[part(me1)], all_buf.at[part(me1)], (send3, recv3), k - 1, peer1(k)[1])
        )

    halo_copies[6].wait_recv()
    halo_copies[7].wait_recv()

    def back(code, value):
        plain = value.astype(F32)
        return jnp.where((code == 1) | (code == 2), flip(perm_s, value), plain)

    from_east = [back(q[0], gcol_recv[0, j]) for j in range(m)]
    from_west = [back(q[1], gcol_recv[1, j]) for j in range(m)]

    def pair(east_code, east_value, west_code, west_value):
        return jnp.where(q[0] == east_code, east_value, 0.0) + jnp.where(q[1] == west_code, west_value, 0.0)

    for j in range(m):
        o = m - 1 - j
        hi = S - m + j
        pg[m : m + S, m + hi, :] += pair(0, from_east[j], 2, from_west[o])
        pg[m : m + S, m + j, :] += pair(2, from_east[o], 0, from_west[j])
        pg[m + hi, m : m + S, :] += pair(1, from_east[j], 3, from_west[o])
        pg[m + j, m : m + S, :] += pair(3, from_east[o], 1, from_west[j])

    @pl.loop(0, S // 8)
    def _(i):
        cells = pg[pl.ds(m + i * 8, 8), m : m + S]
        gf_ref[pl.ds(i * 8, 8)] = (cot_ref[pl.ds(i * 8, 8)].astype(F32) + cells).astype(BF16)

    for copy in copies3:
        copy.wait_recv()
    for copy in halo_copies + copies + copies2 + copies3:
        copy.wait_send()
    for k in range(blocks):
        o_in[:, k * 128 : (k + 1) * 128] = all_buf[k * 128 : (k + 1) * 128].astype(F32) * scale
    o_out[...] = all_buf[base : 2 * base].astype(F32) * scale
    o_kern[...] = all_buf[2 * base : 2 * base + taps].astype(F32) * scale


def body(
    state_field, turn_codes, depth_kernel, conv_bias, norm_gain, norm_shift,
    weight_in, bias_in, weight_out, bias_out, layer_scale, cotangent,
):
    n_face, n_tile = lax.axis_size("face"), lax.axis_size("tile")
    n1, n2 = n_face * SUB, n_tile // SUB
    S, C = state_field.shape[0], state_field.shape[2]
    ks = depth_kernel.shape[0]
    m = ks // 2
    hid = weight_in.shape[1]
    taps = -(-ks * ks // 16) * 16
    rows = -(-(2 * hid + taps) // (16 * n1)) * 16
    rim = -(-(S + 2 * m) // 8) * 8
    scale = 1.0 / math.sqrt(S * S * n_face * n_tile)
    vmem = pl.BlockSpec(memory_space=pltpu.VMEM)
    dma = pltpu.SemaphoreType.DMA
    V = pltpu.VMEM
    line = lambda v: v.reshape(1, -1)
    block_out, grad_field, g_in, g_out, g_kern = pl.pallas_call(
        functools.partial(block_kernel, n_face, n_tile, rows, scale, S, ks),
        out_shape=(
            jax.ShapeDtypeStruct(state_field.shape, BF16),
            jax.ShapeDtypeStruct(state_field.shape, BF16),
            jax.ShapeDtypeStruct(weight_in.shape, F32),
            jax.ShapeDtypeStruct(weight_out.shape, F32),
            jax.ShapeDtypeStruct((taps, C), F32),
        ),
        in_specs=[pl.BlockSpec(memory_space=pltpu.SMEM)] + [vmem] * 11,
        out_specs=[vmem] * 5,
        scratch_shapes=[
            V((S + 2 * m, S + 16, C), F32),
            V((ks, S + 2 * m, S, C), F32),
            V((ks, S + 4 * m, rim, C), F32),
            V((S + 2 * m, rim, C), F32),
            V((taps, 8, C), F32),
            V((C, hid), F32),
            V((C, hid), F32),
            V((2, m, S, C), BF16), V((2, m, S, C), BF16),
            V((2, m, S + 16, C), BF16), V((2, m, S + 16, C), BF16),
            V((2, m, 64, C), BF16), V((2, m, 64, C), BF16),
            V((2, m, S, C), BF16), V((2, m, S, C), BF16),
            V((n1 * rows, C), BF16),
            V((n1 - 1, rows, C), BF16),
            V((n2, rows, C), BF16),
            V((n1 * rows, C), BF16),
            dma((8,)), dma((8,)),
            dma((n1 - 1,)), dma((n1 - 1,)), dma((n2 - 1,)), dma((n2 - 1,)), dma((n1 - 1,)), dma((n1 - 1,)),
        ],
        compiler_params=pltpu.CompilerParams(collective_id=0, has_side_effects=True, vmem_limit_bytes=56 << 20),
    )(
        turn_codes.reshape(-1), state_field, cotangent, depth_kernel.reshape(ks * ks, C),
        line(conv_bias), line(norm_gain), line(norm_shift), weight_in, line(bias_in),
        weight_out, line(bias_out), line(layer_scale),
    )
    return (block_out, grad_field, g_in, g_out, g_kern[: ks * ks].reshape(ks, ks, C))


def solution(mesh):
    placed = (
        P("face", "tile", None),
        P("face", "tile", None),
        P(),
        P(),
        P(),
        P(),
        P(),
        P(),
        P(),
        P(),
        P(),
        P("face", "tile", None),
    )
    return jax.shard_map(
        body,
        mesh=mesh,
        in_specs=placed,
        out_specs=(P("face", "tile", None), P("face", "tile", None), P(), P(), P()),
        check_vma=False,
    )
```

time: 268 us -> 55 us (0.21)
  waiting for transfers between devices: 124 us -> 0 us
  Pallas kernels: 0 us -> 46.4 us
  other arithmetic: 45.7 us -> 0 us
  blocking collectives: 38 us -> 0 us
  between operations: 24.9 us -> 0.65 us
  starting transfers between devices: 14.3 us -> 0 us
  matrix products: 9.04 us -> 0 us
  local copies, waits for them, and re-layouts: 11.3 us -> 7.54 us
    psum x1 -> x0, waiting for transfers between devices: 121 us -> none  [body(): lax.psum((grad_in, grad_out, grad_kern), ('face', 'tile'))]
    pallas_call x0 -> x1, Pallas kernels: none -> 46.4 us  [body(): pl.pallas_call(functools.partial(block_kernel, n_face, n_tile, rows, scal...]
    psum x1 -> x0, blocking collectives: 38 us -> none  [body(): lax.psum((grad_in, grad_out, grad_kern), ('face', 'tile'))]
    reduce_sum x6 -> x0, other arithmetic: 21.7 us -> none  [the longest x3 9.93 us: tile_step(): jnp.sum(padded_f[row_off:row_off + tile_side, col_off:col_off + tile_side...]
    another operation x2 -> x0, other arithmetic: 14.4 us -> none
    ppermute x8 -> x0, starting transfers between devices: 14.3 us -> none  [the longest x4 13.1 us: extended(): after = lax.ppermute(initial, axis, down)]
    dot_general x6 -> x0, matrix products: 9.04 us -> none  [the longest x1 2.22 us: tile_step(): jnp.dot(grad_mixed, weight_out.T, preferred_element_type=jnp.float32)]
    slice x7 -> x1, local copies, waits for them, and re-layouts: 4.74 us -> 0.75 us  [body(): g_kern[:ks * ks].reshape(ks, ks, C)]
  transfers between devices with their start and end apart: 9 -> 0, of which waited for: 3 -> 0; matrix products, arithmetic and copies ran while one was open for 3% -> 0% of each run, Pallas kernels for 0% -> 0%
where the time goes in v2:
time: 55 us; the launch traced here: 54.6 us
  Pallas kernels  46.4 us (84%)
  local copies, waits for them, and re-layouts  7.54 us (14%)
  between operations  0.65 us (1%)
    pallas_call x1, Pallas kernels, body(): pl.pallas_call(functools.partial(block_kernel, n_face, n_tile, rows, scal...  46.4 us
    unnamed x10, local copies, waits for them, and re-layouts  4.82 us
    reshape x1, local copies, waits for them, and re-layouts, body(): depth_kernel.reshape(ks * ks, C)  1.36 us

profile of v2, /device:TPU:0, one launch (start us, length us, event | category | flops | bytes accessed | tf_op | source)
XLA Modules:
  0.0 54.6 jit_solution(4852348532667710359)
XLA Ops:
  0.6 1.4 %reshape.38.dk_ref = f32[49,128]{1,0:T(8,128)} reshape(f32[7,7,128]{2,1,0:T(8,128)} %param.14) | data formatting | bytes 50176 | tf_op jit(solution)/shard_map/reshape | solution.py:374
  2.0 46.4 %shard_map.155 = (bf16[48,48,128]{2,1,0:T(8,128)(2,1)}, bf16[48,48,128]{2,1,0:T(8,128)(2,1)}, f32[128,512]{1,0:T(8,128)}, f32[512,128]{1,0:T(8,128)}, f32[64,128]{1,0:T(8,128)}) custom-call(s32[4]{0:T(128)} %bitcast.8, bf16[48,48,128]{2,1,0:T(8,128)(2,1)} %x_ref.1, bf16[48,48,128]{2,1,0:T(8,128)(2,1)} %cot_ref.1, f32[49,128]{1,0:T(8,128)} %reshape.38.dk_ref, ...), custom_call_target="tpu_custom_call" | custom-call | tf_op jit(solution)/shard_map/pallas_call | solution.py:342
  48.4 0.8 %slice.3 = f32[49,128]{1,0:T(8,128)S(1)} slice(f32[64,128]{1,0:T(8,128)} %get-tuple-element.14), slice={[0:49], [0:128]} | slice | bytes 50176 | tf_op jit(solution)/shard_map/slice | solution.py:378
  49.2 0.6 %reshape.45 = f32[7,7,128]{2,1,0:T(8,128)} reshape(f32[49,128]{1,0:T(8,128)S(1)} %slice.3) | data formatting | bytes 50176 | tf_op jit(solution)/shard_map/reshape | solution.py:378
  49.8 0.0 copy-start
  49.8 2.0 %copy.21 = bf16[48,48,128]{2,1,0:T(8,128)(2,1)} copy(bf16[48,48,128]{2,1,0:T(8,128)(2,1)} %get-tuple-element.20) | data formatting | bytes 1179648
  51.8 0.0 copy-done
  51.8 0.0 copy-start.2
  51.8 0.8 %copy.22 = bf16[48,48,128]{2,1,0:T(8,128)(2,1)} copy(bf16[48,48,128]{2,1,0:T(8,128)(2,1)S(1)} %copy-done) | data formatting | bytes 1179648
  52.6 0.3 copy-done.2
  52.9 0.0 copy-start.1
  52.9 0.7 %copy.23 = f32[128,512]{1,0:T(8,128)} copy(f32[128,512]{1,0:T(8,128)S(1)} %copy-done.2) | data formatting | bytes 524288
  53.6 0.3 copy-done.1
  53.9 0.7 %copy.24 = f32[512,128]{1,0:T(8,128)} copy(f32[512,128]{1,0:T(8,128)S(1)} %copy-done.1) | data formatting | bytes 524288
Async XLA Ops:
  49.8 2.0 %copy-start = (bf16[48,48,128]{2,1,0:T(8,128)(2,1)S(1)}, bf16[48,48,128]{2,1,0:T(8,128)(2,1)}, u32[]{:S(2)}) copy-start(bf16[48,48,128]{2,1,0:T(8,128)(2,1)} %get-tuple-element.21) | copy-start | bytes 1769476
  51.8 1.1 %copy-start.2 = (f32[128,512]{1,0:T(8,128)S(1)}, f32[128,512]{1,0:T(8,128)}, u32[]{:S(2)}) copy-start(f32[128,512]{1,0:T(8,128)} %get-tuple-element.22) | copy-start | bytes 786436
  52.9 1.0 %copy-start.1 = (f32[512,128]{1,0:T(8,128)S(1)}, f32[512,128]{1,0:T(8,128)}, u32[]{:S(2)}) copy-start(f32[512,128]{1,0:T(8,128)} %get-tuple-element.23) | copy-start | bytes 786436

commit v3 on v2

--- a/solution.py
+++ b/solution.py
@@ -18,7 +18,7 @@
     n_face, n_tile, rows, scale, side, ks,
     codes, x_ref, cot_ref, dk_ref, cb_ref, gain_ref, shift_ref, win_ref, bin_ref, wout_ref, bout_ref, ls_ref,
     out_ref, gf_ref, o_in, o_out, o_kern,
-    xpad, xs, gs, pg, kacc, acc_in, acc_out,
+    xpad, xs, gs, pg, hold, kacc, acc_in, acc_out,
     col_send, col_recv, row_send, row_recv, grow_send, grow_recv, gcol_send, gcol_recv,
     send_buf, first_buf, second_buf, all_buf,
     halo_s, halo_r, send1, recv1, send2, recv2, send3, recv3,
@@ -141,27 +141,19 @@
     def _(i):
         shifted(m + i * 6, 6)
 
-    halo_copies[2].wait_recv()
-    halo_copies[3].wait_recv()
-    xpad[0:m] = row_recv[0].astype(F32)
-    xpad[m + S :] = row_recv[1].astype(F32)
-    shifted(0, m)
-    shifted(m + S, m)
-
     R = 8
     M = R * S
     contract0 = (((0,), (0,)), ((), ()))
     contract1 = (((1,), (1,)), ((), ()))
 
-    @pl.loop(0, S // R)
-    def _(i):
+    def pointwise(i):
         i0 = i * R
         parts = []
         for s in range(0, R, 4):
             acc = jnp.zeros((4, S, C), F32)
             for a in range(ks):
                 for b in range(ks):
-                    acc = acc + xs[b, pl.ds(i0 + s + a, 4)] * dk_ref[a * ks + b : a * ks + b + 1]
+                    acc = acc + xs[b, pl.ds(i0 + s + a, 4)] * dk_ref[a, b : b + 1]
             parts.append(acc.reshape(4 * S, C))
         conv = jnp.concatenate(parts, axis=0) + cb_ref[...]
         center = conv - jnp.mean(conv, axis=-1, keepdims=True)
@@ -191,16 +183,31 @@
         for b in range(ks):
             gs[b, pl.ds(i0 + 2 * m, R), b : b + S] = g
 
-    def spread(p):
-        acc = jnp.zeros((m, rim, C), F32)
+    @pl.loop(1, S // R - 1)
+    def _(i):
+        pointwise(i)
+
+    halo_copies[2].wait_recv()
+    halo_copies[3].wait_recv()
+    xpad[0:m] = row_recv[0].astype(F32)
+    xpad[m + S :] = row_recv[1].astype(F32)
+    shifted(0, m)
+    shifted(m + S, m)
+
+    @pl.loop(0, 2)
+    def _(e):
+        pointwise(e * (S // R - 1))
+
+    def spread(p, count, first, width):
+        acc = jnp.zeros((count, width, C), F32)
         for a in range(ks):
             for b in range(ks):
-                acc = acc + gs[b, pl.ds(p + 2 * m - a, m)] * dk_ref[a * ks + b : a * ks + b + 1]
-        pg[pl.ds(p, m)] = acc
+                acc = acc + gs[b, pl.ds(p + 2 * m - a, count), first : first + width] * dk_ref[a, b : b + 1]
+        pg[pl.ds(p, count), first : first + width] = acc
 
     @pl.loop(0, 2)
     def _(e):
-        spread(e * (S + m))
+        spread(e * (S + m), m, 0, rim)
 
     gap = jnp.zeros((m, 64 - rim, C), F32)
     grow_send[0] = jnp.concatenate([pg[0:m], gap], axis=1).astype(BF16)
@@ -236,11 +243,35 @@
         other, where = peer1(k)
         copies.append(remote(send_buf.at[part(other)], first_buf.at[k - 1], (send1, recv1), k - 1, where))
 
-    third = S // m // 2
-
-    @pl.loop(0, third)
-    def _(i):
-        spread(m + i * m)
+    @pl.loop(0, S // 12)
+    def _(i):
+        spread(m + i * 12, 12, 0, 8)
+        spread(m + i * 12, 12, rim - 8, 8)
+
+    halo_copies[4].wait_recv()
+    halo_copies[5].wait_recv()
+    perm_r = mirror(rim, 64, wide - 1)
+    for i in range(m):
+        top_turned = flip(perm_r, grow_recv[0, m - 1 - i])
+        end_turned = flip(perm_r, grow_recv[1, m - 1 - i])
+        north = grow_recv[1, i].astype(F32)[:rim]
+        south = grow_recv[0, i].astype(F32)[:rim]
+        hold[i] = jnp.where(q[3] % 2 == 0, north, 0.0) + jnp.where(q[2] % 2 == 1, top_turned, 0.0)
+        hold[m + i] = jnp.where(q[3] % 2 == 1, end_turned, 0.0) + jnp.where(q[2] % 2 == 0, south, 0.0)
+
+    def add_rows(first, width):
+        for start, at in ((m, 0), (S, m)):
+            pg[start : start + m, first : first + width] += hold[at : at + m, first : first + width]
+
+    add_rows(0, 8)
+    add_rows(rim - 8, 8)
+    for j in range(m):
+        gcol_send[0, j] = pg[m : m + S, j, :].astype(BF16)
+        gcol_send[1, j] = pg[m : m + S, S + m + j, :].astype(BF16)
+    halo_copies += [
+        remote(gcol_send.at[0], gcol_recv.at[0], halo, 6, west),
+        remote(gcol_send.at[1], gcol_recv.at[1], halo, 7, east),
+    ]
 
     total = send_buf[part(me1)].astype(F32)
     for k in range(1, n1):
@@ -251,27 +282,11 @@
     for k in range(1, n2):
         copies2.append(remote(second_buf.at[me2], second_buf.at[me2], (send2, recv2), k - 1, peer2(k)))
 
-    @pl.loop(third, S // m)
-    def _(i):
-        spread(m + i * m)
-
-    halo_copies[4].wait_recv()
-    halo_copies[5].wait_recv()
-    perm_r = mirror(rim, 64, wide - 1)
-    for i in range(m):
-        top_turned = flip(perm_r, grow_recv[0, m - 1 - i])
-        end_turned = flip(perm_r, grow_recv[1, m - 1 - i])
-        north = grow_recv[1, i].astype(F32)[:rim]
-        south = grow_recv[0, i].astype(F32)[:rim]
-        pg[m + i] += jnp.where(q[3] % 2 == 0, north, 0.0) + jnp.where(q[2] % 2 == 1, top_turned, 0.0)
-        pg[S + i] += jnp.where(q[3] % 2 == 1, end_turned, 0.0) + jnp.where(q[2] % 2 == 0, south, 0.0)
-    for j in range(m):
-        gcol_send[0, j] = pg[m : m + S, j, :].astype(BF16)
-        gcol_send[1, j] = pg[m : m + S, S + m + j, :].astype(BF16)
-    halo_copies += [
-        remote(gcol_send.at[0], gcol_recv.at[0], halo, 6, west),
-        remote(gcol_send.at[1], gcol_recv.at[1], halo, 7, east),
-    ]
+    middle = S // 8
+
+    @pl.loop(0, middle)
+    def _(i):
+        spread(m + i * 4, 4, 8, rim - 16)
 
     for copy in copies2:
         copy.wait_recv()
@@ -285,6 +300,11 @@
             remote(all_buf.at[part(me1)], all_buf.at[part(me1)], (send3, recv3), k - 1, peer1(k)[1])
         )
 
+    @pl.loop(middle, S // 4)
+    def _(i):
+        spread(m + i * 4, 4, 8, rim - 16)
+
+    add_rows(8, rim - 16)
     halo_copies[6].wait_recv()
     halo_copies[7].wait_recv()
 
@@ -318,7 +338,9 @@
     for k in range(blocks):
         o_in[:, k * 128 : (k + 1) * 128] = all_buf[k * 128 : (k + 1) * 128].astype(F32) * scale
     o_out[...] = all_buf[base : 2 * base].astype(F32) * scale
-    o_kern[...] = all_buf[2 * base : 2 * base + taps].astype(F32) * scale
+    kern = all_buf[2 * base : 2 * base + taps].astype(F32) * scale
+    for a in range(ks):
+        o_kern[a] = kern[a * ks : (a + 1) * ks]
 
 
 def body(
@@ -346,7 +368,7 @@
             jax.ShapeDtypeStruct(state_field.shape, BF16),
             jax.ShapeDtypeStruct(weight_in.shape, F32),
             jax.ShapeDtypeStruct(weight_out.shape, F32),
-            jax.ShapeDtypeStruct((taps, C), F32),
+            jax.ShapeDtypeStruct(depth_kernel.shape, F32),
         ),
         in_specs=[pl.BlockSpec(memory_space=pltpu.SMEM)] + [vmem] * 11,
         out_specs=[vmem] * 5,
@@ -355,6 +377,7 @@
             V((ks, S + 2 * m, S, C), F32),
             V((ks, S + 4 * m, rim, C), F32),
             V((S + 2 * m, rim, C), F32),
+            V((2 * m, rim, C), F32),
             V((taps, 8, C), F32),
             V((C, hid), F32),
             V((C, hid), F32),
@@ -371,11 +394,11 @@
         ],
         compiler_params=pltpu.CompilerParams(collective_id=0, has_side_effects=True, vmem_limit_bytes=56 << 20),
     )(
-        turn_codes.reshape(-1), state_field, cotangent, depth_kernel.reshape(ks * ks, C),
+        turn_codes.reshape(-1), state_field, cotangent, depth_kernel,
         line(conv_bias), line(norm_gain), line(norm_shift), weight_in, line(bias_in),
         weight_out, line(bias_out), line(layer_scale),
     )
-    return (block_out, grad_field, g_in, g_out, g_kern[: ks * ks].reshape(ks, ks, C))
+    return (block_out, grad_field, g_in, g_out, g_kern)
 
 
 def solution(mesh):

time: 55 us -> 50.6 us (0.920)
  Pallas kernels: 46.4 us -> 44.1 us
  local copies, waits for them, and re-layouts: 7.54 us -> 5.47 us
    pallas_call x1, Pallas kernels: 46.4 us -> 44.1 us  [body(): pl.pallas_call(functools.partial(block_kernel, n_face, n_tile, rows, scal...]
    reshape x2 -> x0, local copies, waits for them, and re-layouts: 1.97 us -> none  [the longest x1 1.36 us: body(): depth_kernel.reshape(ks * ks, C)]
    slice x1 -> x0, local copies, waits for them, and re-layouts: 0.75 us -> none  [body(): g_kern[:ks * ks].reshape(ks, ks, C)]
    unnamed x10 -> x13, local copies, waits for them, and re-layouts: 4.82 us -> 5.47 us
where the time goes in v3:
time: 50.6 us; the launch traced here: 50.3 us
  Pallas kernels  44.1 us (87%)
  local copies, waits for them, and re-layouts  5.47 us (11%)
  between operations  0.66 us (1%)
    pallas_call x1, Pallas kernels, body(): pl.pallas_call(functools.partial(block_kernel, n_face, n_tile, rows, scal...  44.1 us
    unnamed x13, local copies, waits for them, and re-layouts  5.47 us

profile of v3, /device:TPU:0, one launch (start us, length us, event | category | flops | bytes accessed | tf_op | source)
XLA Modules:
  0.0 50.3 jit_solution(7630949972889450674)
XLA Ops:
  0.6 44.1 %shard_map.155 = (bf16[48,48,128]{2,1,0:T(8,128)(2,1)}, bf16[48,48,128]{2,1,0:T(8,128)(2,1)}, f32[128,512]{1,0:T(8,128)}, f32[512,128]{1,0:T(8,128)}, f32[7,7,128]{2,1,0:T(8,128)}) custom-call(s32[4]{0:T(128)} %bitcast.8, bf16[48,48,128]{2,1,0:T(8,128)(2,1)} %x_ref.1, bf16[48,48,128]{2,1,0:T(8,128)(2,1)} %cot_ref.1, f32[7,7,128]{2,1,0:T(8,128)} %dk_ref.1, ...), custom_call_target="tpu_custom_call" | custom-call | tf_op jit(solution)/shard_map/pallas_call | solution.py:364
  44.8 0.0 copy-start
  44.8 2.0 %copy.22 = bf16[48,48,128]{2,1,0:T(8,128)(2,1)} copy(bf16[48,48,128]{2,1,0:T(8,128)(2,1)} %get-tuple-element.10) | data formatting | bytes 1179648
  46.8 0.0 copy-done
  46.8 0.0 copy-start.2
  46.8 0.8 %copy.23 = bf16[48,48,128]{2,1,0:T(8,128)(2,1)} copy(bf16[48,48,128]{2,1,0:T(8,128)(2,1)S(1)} %copy-done) | data formatting | bytes 1179648
  47.6 0.3 copy-done.2
  47.9 0.0 copy-start.1
  47.9 0.7 %copy.24 = f32[128,512]{1,0:T(8,128)} copy(f32[128,512]{1,0:T(8,128)S(1)} %copy-done.2) | data formatting | bytes 524288
  48.6 0.3 copy-done.1
  48.9 0.0 copy-start.3
  48.9 0.7 %copy.25 = f32[512,128]{1,0:T(8,128)} copy(f32[512,128]{1,0:T(8,128)S(1)} %copy-done.1) | data formatting | bytes 524288
  49.6 0.0 copy-done.3
  49.7 0.6 %copy.26 = f32[7,7,128]{2,1,0:T(8,128)} copy(f32[7,7,128]{2,1,0:T(8,128)S(1)} %copy-done.3) | data formatting | bytes 50176
Async XLA Ops:
  44.8 2.0 %copy-start = (bf16[48,48,128]{2,1,0:T(8,128)(2,1)S(1)}, bf16[48,48,128]{2,1,0:T(8,128)(2,1)}, u32[]{:S(2)}) copy-start(bf16[48,48,128]{2,1,0:T(8,128)(2,1)} %get-tuple-element.11) | copy-start | bytes 1769476
  46.8 1.1 %copy-start.2 = (f32[128,512]{1,0:T(8,128)S(1)}, f32[128,512]{1,0:T(8,128)}, u32[]{:S(2)}) copy-start(f32[128,512]{1,0:T(8,128)} %get-tuple-element.12) | copy-start | bytes 786436
  47.9 1.0 %copy-start.1 = (f32[512,128]{1,0:T(8,128)S(1)}, f32[512,128]{1,0:T(8,128)}, u32[]{:S(2)}) copy-start(f32[512,128]{1,0:T(8,128)} %get-tuple-element.13) | copy-start | bytes 786436
  48.9 0.7 %copy-start.3 = (f32[7,7,128]{2,1,0:T(8,128)S(1)}, f32[7,7,128]{2,1,0:T(8,128)}, u32[]{:S(2)}) copy-start(f32[7,7,128]{2,1,0:T(8,128)} %get-tuple-element.14) | copy-start | bytes 75268

commit v4 on v3

--- a/solution.py
+++ b/solution.py
@@ -336,8 +336,8 @@
     for copy in halo_copies + copies + copies2 + copies3:
         copy.wait_send()
     for k in range(blocks):
-        o_in[:, k * 128 : (k + 1) * 128] = all_buf[k * 128 : (k + 1) * 128].astype(F32) * scale
-    o_out[...] = all_buf[base : 2 * base].astype(F32) * scale
+        o_in[:, k * 128 : (k + 1) * 128] = all_buf[k * 128 : (k + 1) * 128]
+    o_out[...] = all_buf[base : 2 * base]
     kern = all_buf[2 * base : 2 * base + taps].astype(F32) * scale
     for a in range(ks):
         o_kern[a] = kern[a * ks : (a + 1) * ks]
@@ -366,8 +366,8 @@
         out_shape=(
             jax.ShapeDtypeStruct(state_field.shape, BF16),
             jax.ShapeDtypeStruct(state_field.shape, BF16),
-            jax.ShapeDtypeStruct(weight_in.shape, F32),
-            jax.ShapeDtypeStruct(weight_out.shape, F32),
+            jax.ShapeDtypeStruct(weight_in.shape, BF16),
+            jax.ShapeDtypeStruct(weight_out.shape, BF16),
             jax.ShapeDtypeStruct(depth_kernel.shape, F32),
         ),
         in_specs=[pl.BlockSpec(memory_space=pltpu.SMEM)] + [vmem] * 11,
@@ -398,7 +398,7 @@
         line(conv_bias), line(norm_gain), line(norm_shift), weight_in, line(bias_in),
         weight_out, line(bias_out), line(layer_scale),
     )
-    return (block_out, grad_field, g_in, g_out, g_kern)
+    return (block_out, grad_field, g_in.astype(F32) * scale, g_out.astype(F32) * scale, g_kern)
 
 
 def solution(mesh):

time: 50.6 us -> 51 us (level)
  other arithmetic: 0 us -> 3.33 us
  local copies, waits for them, and re-layouts: 5.47 us -> 2.71 us
    mul x0 -> x2, other arithmetic: none -> 3.33 us  [the longest x1 1.69 us: body(): g_out.astype(F32) * scale]
    unnamed x13 -> x9, local copies, waits for them, and re-layouts: 5.47 us -> 2.71 us
where the time goes in v4:
time: 51 us; the launch traced here: 50.7 us
  Pallas kernels  44 us (86%)
  other arithmetic  3.33 us (7%)
  local copies, waits for them, and re-layouts  2.71 us (5%)
  between operations  0.66 us (1%)
    pallas_call x1, Pallas kernels, body(): pl.pallas_call(functools.partial(block_kernel, n_face, n_tile, rows, scal...  44 us
    unnamed x9, local copies, waits for them, and re-layouts  2.71 us
    mul x1, other arithmetic, body(): g_out.astype(F32) * scale  1.69 us
    mul x1, other arithmetic, body(): g_in.astype(F32) * scale  1.64 us

profile of v4, /device:TPU:0, one launch (start us, length us, event | category | flops | bytes accessed | tf_op | source)
XLA Modules:
  0.0 50.7 jit_solution(9763138476214352934)
XLA Ops:
  0.6 44.0 %shard_map.155 = (bf16[48,48,128]{2,1,0:T(8,128)(2,1)}, bf16[48,48,128]{2,1,0:T(8,128)(2,1)}, bf16[128,512]{1,0:T(8,128)(2,1)}, bf16[512,128]{1,0:T(8,128)(2,1)}, f32[7,7,128]{2,1,0:T(8,128)}) custom-call(s32[4]{0:T(128)} %bitcast.8, bf16[48,48,128]{2,1,0:T(8,128)(2,1)} %x_ref.1, bf16[48,48,128]{2,1,0:T(8,128)(2,1)} %cot_ref.1, f32[7,7,128]{2,1,0:T(8,128)} %dk_ref.1, ...), custom_call_target="tpu_custom_call" | custom-call | tf_op jit(solution)/shard_map/pallas_call | solution.py:364
  44.7 0.0 copy-start.1
  44.7 1.7 %convert_multiply_fusion = f32[512,128]{1,0:T(8,128)} fusion(bf16[512,128]{1,0:T(8,128)(2,1)} %get-tuple-element.13), kind=kLoop, calls=%fused_computation | loop fusion | flops 131072 | bytes 393216 | tf_op jit(solution)/shard_map/mul | solution.py:401
  46.4 1.6 %convert_multiply_fusion.1 = f32[128,512]{1,0:T(8,128)} fusion(bf16[128,512]{1,0:T(8,128)(2,1)} %get-tuple-element.12), kind=kLoop, calls=%fused_computation.1 | loop fusion | flops 131072 | bytes 393216 | tf_op jit(solution)/shard_map/mul | solution.py:401
  48.0 0.0 copy-done.1
  48.0 0.0 copy-start
  48.0 0.8 %copy.20 = bf16[48,48,128]{2,1,0:T(8,128)(2,1)} copy(bf16[48,48,128]{2,1,0:T(8,128)(2,1)S(1)} %copy-done.1) | data formatting | bytes 1179648
  48.8 0.5 copy-done
  49.3 0.0 copy-start.2
  49.3 0.8 %copy.21 = bf16[48,48,128]{2,1,0:T(8,128)(2,1)} copy(bf16[48,48,128]{2,1,0:T(8,128)(2,1)S(1)} %copy-done) | data formatting | bytes 1179648
  50.1 0.0 copy-done.2
  50.1 0.6 %copy.22 = f32[7,7,128]{2,1,0:T(8,128)} copy(f32[7,7,128]{2,1,0:T(8,128)S(1)} %copy-done.2) | data formatting | bytes 50176
Async XLA Ops:
  44.7 3.3 %copy-start.1 = (bf16[48,48,128]{2,1,0:T(8,128)(2,1)S(1)}, bf16[48,48,128]{2,1,0:T(8,128)(2,1)}, u32[]{:S(2)}) copy-start(bf16[48,48,128]{2,1,0:T(8,128)(2,1)} %get-tuple-element.20) | copy-start | bytes 1769476
  48.0 1.3 %copy-start = (bf16[48,48,128]{2,1,0:T(8,128)(2,1)S(1)}, bf16[48,48,128]{2,1,0:T(8,128)(2,1)}, u32[]{:S(2)}) copy-start(bf16[48,48,128]{2,1,0:T(8,128)(2,1)} %get-tuple-element.21) | copy-start | bytes 1769476
  49.3 0.8 %copy-start.2 = (f32[7,7,128]{2,1,0:T(8,128)S(1)}, f32[7,7,128]{2,1,0:T(8,128)}, u32[]{:S(2)}) copy-start(f32[7,7,128]{2,1,0:T(8,128)} %get-tuple-element.24) | copy-start | bytes 75268
